TPU v7x, 32 devices: a whole 2x2x4 slice. The times are simulated.
32 devices in a mesh: dp: 1, seq: 32 (over z, y, x, core).
Axes of the slice: x: 2, y: 2, z: 4, core: 2. Of those that a mesh axis runs over, the one named last changes fastest.
Arguments:
- tokens: bfloat16 [1, 128, 512, 384], P('dp', 'seq'), may hold values from -6 to 6
- cotangent: bfloat16 [1, 128, 512, 384], P('dp', 'seq'), may hold values from -6 to 6
- wqkv_spatial: bfloat16 [384, 1152], replicated, may hold values from -12.5 to 12.5
- wo_spatial: bfloat16 [384, 384], replicated, may hold values from -0.3125 to 0.3125
- wqkv_temporal: bfloat16 [384, 1152], replicated, may hold values from -12.5 to 12.5
- wo_temporal: bfloat16 [384, 384], replicated, may hold values from -0.3125 to 0.3125
Outputs:
- token_grad: bfloat16 [1, 128, 512, 384], P('dp', 'seq')
- grad_wqkv_spatial: float32 [384, 1152], P(None, 'seq')
- grad_wo_spatial: float32 [384, 384], P(None, 'seq')
- grad_wqkv_temporal: float32 [384, 1152], P(None, 'seq')
- grad_wo_temporal: float32 [384, 384], P(None, 'seq')
All inputs are finite; a program needn't handle non-finite values.
Results may differ from a plain program's by a relative error of at most 0.015.
Values may be sent and summed in bfloat16 or wider, within the bound.
A program may use at most 128 MiB of HBM per device.

v0:
```python
import jax
import jax.numpy as jnp
from jax import lax
from jax.sharding import PartitionSpec as P

HEADS = 6


def product(pattern, left, right):
    return jnp.einsum(pattern, left, right, preferred_element_type=jnp.float32)


def normalize(values):
    average = jnp.mean(values, -1, keepdims=True)
    centered = values - average
    spread = jnp.mean(centered * centered, -1, keepdims=True)
    inverse = lax.rsqrt(spread + 1e-06)
    return (centered * inverse, inverse)


def normalize_back(scaled, inverse, upstream):
    return inverse * (
        upstream
        - jnp.mean(upstream, -1, keepdims=True)
        - scaled * jnp.mean(upstream * scaled, -1, keepdims=True)
    )


def patterns(layout):
    key_layout = layout.replace("s", "t")
    batch_letters = "".join((letter for letter in layout if letter not in "she"))
    return (key_layout, batch_letters + "hst")


def attend_block(queries, key_rows, values, layout):
    key_layout, score_layout = patterns(layout)
    factor = queries.shape[-1] ** (-0.5)
    scores = product(layout + "," + key_layout + "->" + score_layout, queries, key_rows) * factor
    probs = jax.nn.softmax(scores, axis=-1).astype(jnp.bfloat16)
    output = product(score_layout + "," + key_layout + "->" + layout, probs, values).astype(
        jnp.bfloat16
    )
    return (output, probs)


def attend_grad(queries, key_rows, values, upstream, probs, layout):
    key_layout, score_layout = patterns(layout)
    factor = queries.shape[-1] ** (-0.5)
    prob_grad = product(layout + "," + key_layout + "->" + score_layout, upstream, values)
    weights = probs.astype(jnp.float32)
    score_grad = (
        weights * (prob_grad - jnp.sum(weights * prob_grad, -1, keepdims=True)) * factor
    ).astype(jnp.bfloat16)
    query_grad = product(score_layout + "," + key_layout + "->" + layout, score_grad, key_rows)
    key_grad = product(score_layout + "," + layout + "->" + key_layout, score_grad, queries)
    value_grad = product(score_layout + "," + layout + "->" + key_layout, probs, upstream)
    return (query_grad, key_grad, value_grad)


def split_heads(combined):
    shape = combined.shape
    parted = combined.reshape(shape[:-1] + (3, HEADS, shape[-1] // (3 * HEADS)))
    return (parted[..., 0, :, :], parted[..., 1, :, :], parted[..., 2, :, :])


def frame_rows(tensor):
    return tensor.reshape((-1,) + tensor.shape[2:])


def on_device(tokens, cotangent, wqkv_spatial, wo_spatial, wqkv_temporal, wo_temporal):
    clip_count, frame_local, patch_count, model_width = tokens.shape
    head_width = model_width // HEADS
    block_rows = min(512, patch_count)
    inputs = tokens.astype(jnp.float32)
    scaled_s, inverse_s = normalize(inputs)
    normed_s = scaled_s.astype(jnp.bfloat16)
    combined_s = jnp.dot(normed_s, wqkv_spatial, preferred_element_type=jnp.float32).astype(
        jnp.bfloat16
    )
    queries_s, keys_s, values_s = [frame_rows(member) for member in split_heads(combined_s)]
    output, probs = attend_block(queries_s, keys_s, values_s, "bshe")
    outputs_s = [output]
    probs_s = [probs]
    attended_s = jnp.concatenate(outputs_s, 1).reshape(tokens.shape)
    stream = (inputs + jnp.dot(attended_s, wo_spatial, preferred_element_type=jnp.float32)).astype(
        jnp.bfloat16
    )
    stream_t, upstream_out = (
        lax.all_to_all(stream, "seq", split_axis=2, concat_axis=1, tiled=True),
        lax.all_to_all(cotangent, "seq", split_axis=2, concat_axis=1, tiled=True),
    )
    scaled_t, inverse_t = normalize(stream_t.astype(jnp.float32))
    normed_t = scaled_t.astype(jnp.bfloat16)
    combined_t = jnp.dot(normed_t, wqkv_temporal, preferred_element_type=jnp.float32).astype(
        jnp.bfloat16
    )
    queries_t, keys_t, values_t = split_heads(combined_t)
    attended_t, probs_t = attend_block(queries_t, keys_t, values_t, "csphe")
    attended_t = attended_t.reshape(stream_t.shape)
    factor = (
        clip_count * frame_local * patch_count * lax.axis_size("dp") * lax.axis_size("seq")
    ) ** (-0.5)
    grad_wo_t = product("cfpd,cfpe->de", attended_t, upstream_out) * factor
    head_grad_t = (
        product("cfpe,de->cfpd", upstream_out, wo_temporal)
        .astype(jnp.bfloat16)
        .reshape(queries_t.shape)
    )
    query_grad, key_grad, value_grad = attend_grad(
        queries_t, keys_t, values_t, head_grad_t, probs_t, "csphe"
    )
    combined_grad_t = (
        jnp.concatenate([query_grad, key_grad, value_grad], 3)
        .astype(jnp.bfloat16)
        .reshape(combined_t.shape)
    )
    grad_wqkv_t = product("cfpd,cfpe->de", normed_t, combined_grad_t) * factor
    input_grad_t = product("cfpe,de->cfpd", combined_grad_t, wqkv_temporal)
    branch_t = normalize_back(scaled_t, inverse_t, input_grad_t).astype(jnp.bfloat16)
    branch_s = lax.all_to_all(branch_t, "seq", split_axis=1, concat_axis=2, tiled=True)
    stream_grad = (cotangent.astype(jnp.float32) + branch_s.astype(jnp.float32)).astype(
        jnp.bfloat16
    )
    grad_wo_s = product("cfpd,cfpe->de", attended_s, stream_grad) * factor
    head_grad_s = frame_rows(
        product("cfpe,de->cfpd", stream_grad, wo_spatial)
        .astype(jnp.bfloat16)
        .reshape(tokens.shape[:3] + (HEADS, head_width))
    )
    key_total = jnp.zeros(keys_s.shape, jnp.float32)
    value_total = jnp.zeros(values_s.shape, jnp.float32)
    query_parts = []
    for number, offset in enumerate(range(0, patch_count, block_rows)):
        query_grad, key_grad, value_grad = attend_grad(
            queries_s, keys_s, values_s, head_grad_s, probs_s[number], "bshe"
        )
        query_parts.append(query_grad)
        key_total = key_total + key_grad
        value_total = value_total + value_grad
    combined_grad_s = jnp.concatenate([jnp.concatenate(query_parts, 1), key_total, value_total], 2)
    combined_grad_s = combined_grad_s.astype(jnp.bfloat16).reshape(combined_s.shape)
    grad_wqkv_s = product("cfpd,cfpe->de", normed_s, combined_grad_s) * factor
    input_grad_s = product("cfpe,de->cfpd", combined_grad_s, wqkv_spatial)
    token_grad = (
        stream_grad.astype(jnp.float32) + normalize_back(scaled_s, inverse_s, input_grad_s)
    ).astype(jnp.bfloat16)
    gradients = (grad_wqkv_s, grad_wo_s, grad_wqkv_t, grad_wo_t)
    summed = (
        lax.psum(gradients[0].astype(jnp.bfloat16), "dp").astype(jnp.float32),
        lax.psum(gradients[1].astype(jnp.bfloat16), "dp").astype(jnp.float32),
        lax.psum(gradients[2].astype(jnp.bfloat16), "dp").astype(jnp.float32),
        lax.psum(gradients[3].astype(jnp.bfloat16), "dp").astype(jnp.float32),
    )
    shares = (
        lax.psum_scatter(summed[0], "seq", scatter_dimension=1, tiled=True),
        lax.psum_scatter(summed[1], "seq", scatter_dimension=1, tiled=True),
        lax.psum_scatter(summed[2], "seq", scatter_dimension=1, tiled=True),
        lax.psum_scatter(summed[3], "seq", scatter_dimension=1, tiled=True),
    )
    return (token_grad, shares[0], shares[1], shares[2], shares[3])


def solution(mesh):
    in_specs = (P("dp", "seq", None, None), P("dp", "seq", None, None), P(), P(), P(), P())
    out_specs = (
        P("dp", "seq", None, None),
        P(None, "seq"),
        P(None, "seq"),
        P(None, "seq"),
        P(None, "seq"),
    )
    return jax.shard_map(
        on_device, mesh=mesh, in_specs=in_specs, out_specs=out_specs, check_vma=False
    )
```

profile of v0, /device:TPU:0, one launch (start us, length us, event | category | flops | bytes accessed | tf_op | source)
XLA Modules:
  0.0 506.7 jit_solution(7537777595587474917)
XLA Ops:
  4.8 4.6 convolution_convert_fusion.1
  9.4 6.6 %copy.154 = bf16[4,512,1152]{1,2,0:T(8,128)(2,1)} copy(bf16[4,512,1152]{2,1,0:T(8,128)(2,1)} %convolution_convert_fusion.1) | data formatting | bytes 9437184 | tf_op jit(solution)/shard_map/convert_element_type | solution.py:77
  16.0 14.3 %fusion.104 = (f32[4,6,512]{2,1,0:T(8,128)S(1)}, f32[4,6,512,512]{2,3,1,0:T(8,128)}) fusion(bf16[1,4,512,3,6,64]{2,5,4,3,1,0:T(8,128)(2,1)} %bitcast.227), kind=kOutput, calls=%fused_computation.135 | convolution fusion | flops 824181248 | bytes 28360704 | tf_op jit(solution)/shard_map/sub | solution.py:39
  30.3 10.2 %divide_convert_fusion = bf16[4,6,512,512]{2,3,1,0:T(8,128)(2,1)S(1)} fusion(f32[4,6,512,512]{2,3,1,0:T(8,128)} %get-tuple-element.18, f32[4,6,512]{2,1,0:T(8,128)S(1)} %get-tuple-element.17), kind=kLoop, calls=%fused_computation.8 | loop fusion | flops 12582912 | bytes 37797888 | tf_op jit(solution)/shard_map/convert_element_type | solution.py:39
  40.5 4.8 convolution_convert_fusion.4
  48.9 7.3 %all-to-all-start = ((bf16[1,4,512,384]{3,1,0,2:T(4,128)(2,1)}), bf16[1,4,512,384]{3,1,0,2:T(4,128)(2,1)S(1)}, u32[]{:S(2)}, u32[]{:S(2)}) async-start(bf16[1,4,512,384]{3,1,0,2:T(4,128)(2,1)} %copy.160), calls=%async_computation | async-start | bytes 3145728 | tf_op jit(solution)/shard_map/all_to_all | solution.py:89
  56.2 3.8 copy.170
  60.0 33.9 %all-to-all-done = bf16[1,4,512,384]{3,1,0,2:T(4,128)(2,1)S(1)} async-done(((bf16[1,4,512,384]{3,1,0,2:T(4,128)(2,1)}), bf16[1,4,512,384]{3,1,0,2:T(4,128)(2,1)S(1)}, u32[]{:S(2)}, u32[]{:S(2)}) %all-to-all-start) | async-done | bytes 1572896 | tf_op jit(solution)/shard_map/all_to_all | solution.py:89
  93.9 4.1 all-to-all-start.1
  101.7 5.6 %copy.164 = f32[1,32,4,16,384]{4,2,1,3,0:T(4,128)} copy(f32[1,32,4,16,384]{4,3,1,2,0:T(8,128)} %get-tuple-element.16) | data formatting | bytes 6291456 | tf_op jit(solution)/shard_map/convert_element_type | solution.py:92
  107.3 4.9 reshape.352
  112.2 7.0 %convolution_convert_fusion = bf16[128,16,1152]{2,0,1:T(8,128)(2,1)} fusion(f32[128,16,384]{2,0,1:T(8,128)} %reshape.352, f32[128,16]{0,1:T(8,128)S(1)} %copy.166, f32[128,16]{0,1:T(8,128)S(1)} %copy.163, bf16[384,1152]{1,0:T(8,128)(2,1)S(1)} %copy-done), kind=kOutput, calls=%fused_computation.26 | convolution fusion | flops 1816657920 | bytes 8765440 | tf_op jit(solution)/shard_map/dot_general | solution.py:94
  119.2 6.6 %copy.167 = bf16[128,16,1152]{0,2,1:T(8,128)(2,1)} copy(bf16[128,16,1152]{2,0,1:T(8,128)(2,1)} %convolution_convert_fusion) | data formatting | bytes 9437184 | tf_op jit(solution)/shard_map/convert_element_type | solution.py:94
  125.8 2.9 fusion.62
  128.8 4.1 fusion.105
  132.9 2.9 all-to-all-done.1
  138.0 11.3 %reshape.347 = bf16[128,16,384]{2,0,1:T(8,128)(2,1)} reshape(bf16[1,32,4,16,384]{4,2,1,3,0:T(4,128)(2,1)S(1)} %bitcast.232) | data formatting | bytes 3145728 | tf_op jit(solution)/shard_map/reshape.28
  149.3 3.8 convolution_convert_fusion.3
  153.1 2.8 copy.172
  155.8 5.7 %fusion.63 = f32[16,6,128,128]{2,3,1,0:T(8,128)} fusion(bf16[128,16,6,64]{0,3,2,1:T(8,128)(2,1)} %bitcast.223, bf16[1,128,16,3,6,64]{1,5,4,3,2,0:T(8,128)(2,1)} %bitcast.213), kind=kOutput, calls=%fused_computation.92 | convolution fusion | flops 201326592 | bytes 9437184 | tf_op jit(solution)/shard_map/csphe,ctphe->cphst/dot_general | solution.py:10
  161.5 2.7 divide_convert_fusion.1
  164.2 10.2 %fusion.49 = bf16[1,128,16,6,64]{1,4,3,2,0:T(8,128)(2,1)} fusion(bf16[16,6,128,128]{2,3,1,0:T(8,128)(2,1)} %divide_convert_fusion.1, f32[16,6,128,128]{2,3,1,0:T(8,128)} %fusion.63, bf16[1,128,16,3,6,64]{1,5,4,3,2,0:T(8,128)(2,1)} %bitcast.214), kind=kOutput, calls=%fused_computation.67 | convolution fusion | flops 212349056 | bytes 22020096 | tf_op jit(solution)/shard_map/cphst,ctphe->csphe/dot_general | solution.py:10
  174.4 10.3 %fusion.50 = bf16[1,128,16,6,64]{1,4,3,2,0:T(8,128)(2,1)} fusion(bf16[16,6,128,128]{2,3,1,0:T(8,128)(2,1)} %divide_convert_fusion.1, f32[16,6,128,128]{2,3,1,0:T(8,128)} %fusion.63, bf16[1,128,16,3,6,64]{1,5,4,3,2,0:T(8,128)(2,1)} %bitcast.215), kind=kOutput, calls=%fused_computation.68 | convolution fusion | flops 212349056 | bytes 22020096 | tf_op jit(solution)/shard_map/cphst,csphe->ctphe/dot_general | solution.py:10
  184.7 4.3 convolution_bitcast_fusion.3
  191.8 4.4 fusion.101
  199.6 4.3 all-to-all-start.2
  203.9 7.2 %copy.189 = bf16[128,16,1152]{2,1,0:T(8,128)(2,1)} copy(bf16[128,16,1152]{0,2,1:T(8,128)(2,1)} %bitcast.222) | data formatting | bytes 9437184 | tf_op jit(solution)/shard_map/convert_element_type | solution.py:114
  213.1 2.8 convolution_convert_fusion.5
  216.9 3.9 fusion.42
  220.8 20.9 %all-to-all-done.2 = bf16[1,128,16,384]{3,2,0,1:T(8,128)(2,1)} async-done(((bf16[1,128,16,384]{3,2,0,1:T(8,128)(2,1)}), bf16[1,128,16,384]{3,2,0,1:T(8,128)(2,1)}, u32[]{:S(2)}, u32[]{:S(2)}) %all-to-all-start.2) | async-done | bytes 1572896 | tf_op jit(solution)/shard_map/all_to_all | solution.py:120
  246.8 11.8 %fusion.61 = f32[4,6,512,512]{2,3,1,0:T(8,128)} fusion(bf16[4,512,6,64]{1,3,2,0:T(8,128)(2,1)S(1)} %bitcast.219, bf16[1,4,512,3,6,64]{2,5,4,3,1,0:T(8,128)(2,1)} %bitcast.229), kind=kOutput, calls=%fused_computation.90 | convolution fusion | flops 805306368 | bytes 28311552 | tf_op jit(solution)/shard_map/bshe,bthe->bhst/dot_general | solution.py:10
  258.6 26.9 %fusion.51 = bf16[4,512,6,64]{1,3,2,0:T(8,128)(2,1)} fusion(bf16[4,6,512,512]{2,3,1,0:T(8,128)(2,1)} %copy-done.2, f32[4,6,512,512]{2,3,1,0:T(8,128)} %fusion.61, bf16[1,4,512,3,6,64]{2,5,4,3,1,0:T(8,128)(2,1)} %bitcast.230), kind=kOutput, calls=%fused_computation.69 | convolution fusion | flops 849359360 | bytes 78643200 | tf_op jit(solution)/shard_map/bhst,bthe->bshe/dot_general | solution.py:10
  285.5 27.1 %fusion.52 = bf16[4,512,6,64]{1,3,2,0:T(8,128)(2,1)} fusion(bf16[4,6,512,512]{2,3,1,0:T(8,128)(2,1)} %copy-done.2, f32[4,6,512,512]{2,3,1,0:T(8,128)} %fusion.61, bf16[1,4,512,3,6,64]{2,5,4,3,1,0:T(8,128)(2,1)} %bitcast.231), kind=kOutput, calls=%fused_computation.70 | convolution fusion | flops 849359360 | bytes 78643200 | tf_op jit(solution)/shard_map/bhst,bshe->bthe/dot_general | solution.py:10
  312.6 8.6 %convolution_bitcast_fusion.2 = bf16[4,512,6,64]{1,3,2,0:T(8,128)(2,1)S(1)} fusion(bf16[4,512,6,64]{1,3,2,0:T(8,128)(2,1)S(1)} %bitcast.220, bf16[4,6,512,512]{2,3,1,0:T(8,128)(2,1)} %copy-done.2), kind=kOutput, calls=%fused_computation.66 | convolution fusion | flops 805306368 | bytes 15728640 | tf_op jit(solution)/shard_map/bhst,bshe->bthe/dot_general | solution.py:10
  325.2 4.0 fusion.44
  329.2 82.3 %fusion.102 = (f32[384,48]{0,1:T(8,128)S(1)}, f32[384,16]{0,1:T(8,128)S(1)}, f32[384,48]{0,1:T(8,128)S(1)}, f32[384,16]{0,1:T(8,128)S(1)}) fusion(f32[384,1152]{0,1:T(8,128)} %fusion.44, f32[384,384]{0,1:T(8,128)S(1)} %fusion.75, f32[384,1152]{0,1:T(8,128)} %fusion.42, f32[384,384]{0,1:T(8,128)S(1)} %fusion.78), kind=kCustom, calls=%all-reduce-scatter.4 | all-reduce-scatter fusion | flops 1572866 | bytes 4915200
  415.4 6.5 %fusion.106 = (f32[4,512]{1,0:T(4,128)S(1)}, f32[4,512,384]{1,2,0:T(8,128)}) fusion(bf16[4,512,1152]{1,2,0:T(8,128)(2,1)} %bitcast.234, bf16[384,1152]{1,0:T(8,128)(2,1)} %param.8), kind=kOutput, calls=%fused_computation.137 | convolution fusion | flops 1812723712 | bytes 8757248 | tf_op jit(solution)/shard_map/cfpe,de->cfpd/dot_general | solution.py:10
  424.5 3.5 copy.184
  428.0 2.6 fusion.28
  433.0 6.9 %collective-permute-start.28 = (f32[384,16]{0,1:T(8,128)S(1)}, f32[384,16]{0,1:T(8,128)S(1)}, u32[]{:S(2)}, u32[]{:S(2)}) collective-permute-start(f32[384,16]{0,1:T(8,128)S(1)} %get-tuple-element.14), channel_id=1, source_target_pairs={{0,5},{1,6},{2,7},{3,8},{4,9},{5,10},{6,11},{7,12},{8,13},{9,14},{... | collective-permute-start | bytes 73736
  439.9 2.6 collective-permute-start.29
  446.7 2.7 collective-permute-start.11
  451.6 2.8 collective-permute-start.13
  457.2 3.6 collective-permute-start.9
  465.7 2.7 collective-permute-start.16
  470.3 3.4 collective-permute-start.18
  489.8 3.0 collective-permute-start.2
  498.2 3.1 collective-permute-start.5
  (158 shorter events, 82.6 us)
Async XLA Ops:
  0.6 111.6 %copy-start = (bf16[384,1152]{1,0:T(8,128)(2,1)S(1)}, bf16[384,1152]{1,0:T(8,128)(2,1)}, u32[]{:S(2)}) copy-start(bf16[384,1152]{1,0:T(8,128)(2,1)} %param.10) | copy-start | bytes 2654212
  48.9 45.0 %all-to-all-start = ((bf16[1,4,512,384]{3,1,0,2:T(4,128)(2,1)}), bf16[1,4,512,384]{3,1,0,2:T(4,128)(2,1)S(1)}, u32[]{:S(2)}, u32[]{:S(2)}) async-start(bf16[1,4,512,384]{3,1,0,2:T(4,128)(2,1)} %copy.160), calls=%async_computation | async-start | bytes 3145728 | tf_op jit(solution)/shard_map/all_to_all | solution.py:89
  93.9 6.2 %copy-start.8 = (bf16[1,4,512,384]{3,1,0,2:T(4,128)(2,1)}, bf16[1,4,512,384]{3,1,0,2:T(4,128)(2,1)S(1)}, u32[]{:S(2)}) copy-start(bf16[1,4,512,384]{3,1,0,2:T(4,128)(2,1)S(1)} %all-to-all-done) | copy-start | bytes 4718596
  93.9 41.9 %all-to-all-start.1 = ((bf16[1,4,512,384]{3,1,0,2:T(4,128)(2,1)}), bf16[1,4,512,384]{3,1,0,2:T(4,128)(2,1)}, u32[]{:S(2)}, u32[]{:S(2)}) async-start(bf16[1,4,512,384]{3,1,0,2:T(4,128)(2,1)} %copy.170), calls=%async_computation.1 | async-start | bytes 3145728 | tf_op jit(solution)/shard_map/all_to_all | solution.py:90
  135.8 13.5 %copy-start.22 = (bf16[384,384]{1,0:T(8,128)(2,1)S(1)}, bf16[384,384]{1,0:T(8,128)(2,1)}, u32[]{:S(2)}) copy-start(bf16[384,384]{1,0:T(8,128)(2,1)} %param.11) | copy-start | bytes 884740
  153.1 8.4 %slice-start = ((s8[6291456]{0:T(1024)(128)(4,1)}), s8[2097152]{0:T(1024)(128)(4,1)S(1)}, s32[]{:S(2)}) async-start(s8[6291456]{0:T(1024)(128)(4,1)} %bitcast.217), calls=%async_computation.3 | async-start | bytes 4194304
  155.8 5.7 %slice-start.1 = ((s8[6291456]{0:T(1024)(128)(4,1)}), s8[4194304]{0:T(1024)(128)(4,1)S(1)}, s32[]{:S(2)}) async-start(s8[6291456]{0:T(1024)(128)(4,1)} %bitcast.217), calls=%async_computation.4 | async-start | bytes 8388608
  174.4 10.3 %copy-start.10 = (bf16[128,16,384]{0,2,1:T(8,128)(2,1)S(1)}, bf16[128,16,384]{0,2,1:T(8,128)(2,1)}, u32[]{:S(2)}) copy-start(bf16[128,16,384]{0,2,1:T(8,128)(2,1)} %copy.172) | copy-start | bytes 4718596
  189.6 6.6 %copy-start.7 = (bf16[1,128,16,18,64]{1,4,3,2,0:T(8,128)(2,1)}, bf16[1,128,16,18,64]{1,4,3,2,0:T(8,128)(2,1)S(1)}, u32[]{:S(2)}) copy-start(bf16[1,128,16,18,64]{1,4,3,2,0:T(8,128)(2,1)S(1)} %maximum_convert_fusion) | copy-start | bytes 14155780
  199.6 42.0 %all-to-all-start.2 = ((bf16[1,128,16,384]{3,2,0,1:T(8,128)(2,1)}), bf16[1,128,16,384]{3,2,0,1:T(8,128)(2,1)}, u32[]{:S(2)}, u32[]{:S(2)}) async-start(bf16[1,128,16,384]{3,2,0,1:T(8,128)(2,1)} %copy.178), calls=%async_computation.2 | async-start | bytes 3145728 | tf_op jit(solution)/shard_map/all_to_all | solution.py:120
  203.9 7.3 %copy-start.9 = (bf16[1,4,512,384]{3,1,0,2:T(4,128)(2,1)S(1)}, bf16[1,4,512,384]{3,1,0,2:T(4,128)(2,1)}, u32[]{:S(2)}) copy-start(bf16[1,4,512,384]{3,1,0,2:T(4,128)(2,1)} %copy-done.8) | copy-start | bytes 4718596
  220.8 22.5 %copy-start.14 = (bf16[1,4,512,384]{3,2,1,0:T(8,128)(2,1)S(1)}, bf16[1,4,512,384]{3,2,1,0:T(8,128)(2,1)}, u32[]{:S(2)}) copy-start(bf16[1,4,512,384]{3,2,1,0:T(8,128)(2,1)} %param.7) | copy-start | bytes 4718596
  312.6 8.6 %copy-start.17 = (bf16[4,512,6,64]{1,3,2,0:T(8,128)(2,1)S(1)}, bf16[4,512,6,64]{1,3,2,0:T(8,128)(2,1)}, u32[]{:S(2)}) copy-start(bf16[4,512,6,64]{1,3,2,0:T(8,128)(2,1)} %fusion.51) | copy-start | bytes 4718596
  411.5 28.4 %collective-permute-start.24 = (f32[384,16]{0,1:T(8,128)S(1)}, f32[384,16]{0,1:T(8,128)S(1)}, u32[]{:S(2)}, u32[]{:S(2)}) collective-permute-start(f32[384,16]{0,1:T(8,128)S(1)} %get-tuple-element.14), channel_id=1, source_target_pairs={{0,1},{1,2},{2,3},{3,4},{4,5},{5,6},{6,7},{7,8},{8,9},{9,10},{10,1... | collective-permute-start | bytes 73736
  412.8 29.8 %collective-permute-start.25 = (f32[384,16]{0,1:T(8,128)S(1)}, f32[384,16]{0,1:T(8,128)S(1)}, u32[]{:S(2)}, u32[]{:S(2)}) collective-permute-start(f32[384,16]{0,1:T(8,128)S(1)} %get-tuple-element.14), channel_id=1, source_target_pairs={{0,2},{1,3},{2,4},{3,5},{4,6},{5,7},{6,8},{7,9},{8,10},{9,11},{10,... | collective-permute-start | bytes 73736
  414.1 30.8 %collective-permute-start.26 = (f32[384,16]{0,1:T(8,128)S(1)}, f32[384,16]{0,1:T(8,128)S(1)}, u32[]{:S(2)}, u32[]{:S(2)}) collective-permute-start(f32[384,16]{0,1:T(8,128)S(1)} %get-tuple-element.14), channel_id=1, source_target_pairs={{0,3},{1,4},{2,5},{3,6},{4,7},{5,8},{6,9},{7,10},{8,11},{9,12},{10... | collective-permute-start | bytes 73736
  421.9 8.7 %collective-permute-start.31 = (f32[384,12]{0,1:T(8,128)S(1)}, f32[384,12]{0,1:T(8,128)S(1)}, u32[]{:S(2)}, u32[]{:S(2)}) collective-permute-start(f32[384,12]{0,1:T(8,128)S(1)} %slice.33), channel_id=1, source_target_pairs={{0,8},{1,9},{2,10},{3,11},{4,12},{5,13},{6,14},{7,15},{8,16},{9,17... | collective-permute-start | bytes 55304
  423.2 9.8 %collective-permute-start.15 = (f32[384,12]{0,1:T(8,128)S(1)}, f32[384,12]{0,1:T(8,128)S(1)}, u32[]{:S(2)}, u32[]{:S(2)}) collective-permute-start(f32[384,12]{0,1:T(8,128)S(1)} %slice.31), channel_id=1, source_target_pairs={{0,8},{1,9},{2,10},{3,11},{4,12},{5,13},{6,14},{7,15},{8,16},{9,17... | collective-permute-start | bytes 55304
  428.0 34.1 %copy-start.3 = (f32[4,512,384]{2,1,0:T(8,128)S(1)}, f32[4,512,384]{2,1,0:T(8,128)}, u32[]{:S(2)}) copy-start(f32[4,512,384]{2,1,0:T(8,128)} %copy.184) | copy-start | bytes 9437188
  428.0 34.1 %copy-start.12 = (bf16[1,4,512,384]{3,2,1,0:T(8,128)(2,1)S(1)}, bf16[1,4,512,384]{3,2,1,0:T(8,128)(2,1)}, u32[]{:S(2)}) copy-start(bf16[1,4,512,384]{3,2,1,0:T(8,128)(2,1)} %copy-done.11) | copy-start | bytes 4718596
  430.6 16.1 %collective-permute-start.27 = (f32[384,16]{0,1:T(8,128)S(1)}, f32[384,16]{0,1:T(8,128)S(1)}, u32[]{:S(2)}, u32[]{:S(2)}) collective-permute-start(f32[384,16]{0,1:T(8,128)S(1)} %get-tuple-element.14), channel_id=1, source_target_pairs={{0,4},{1,5},{2,6},{3,7},{4,8},{5,9},{6,10},{7,11},{8,12},{9,13},{1... | collective-permute-start | bytes 73736
  433.0 16.4 %collective-permute-start.28 = (f32[384,16]{0,1:T(8,128)S(1)}, f32[384,16]{0,1:T(8,128)S(1)}, u32[]{:S(2)}, u32[]{:S(2)}) collective-permute-start(f32[384,16]{0,1:T(8,128)S(1)} %get-tuple-element.14), channel_id=1, source_target_pairs={{0,5},{1,6},{2,7},{3,8},{4,9},{5,10},{6,11},{7,12},{8,13},{9,14},{... | collective-permute-start | bytes 73736
  439.9 11.6 %collective-permute-start.29 = (f32[384,16]{0,1:T(8,128)S(1)}, f32[384,16]{0,1:T(8,128)S(1)}, u32[]{:S(2)}, u32[]{:S(2)}) collective-permute-start(f32[384,16]{0,1:T(8,128)S(1)} %get-tuple-element.14), channel_id=1, source_target_pairs={{0,6},{1,7},{2,8},{3,9},{4,10},{5,11},{6,12},{7,13},{8,14},{9,15},... | collective-permute-start | bytes 73736
  442.6 11.8 %collective-permute-start.30 = (f32[384,16]{0,1:T(8,128)S(1)}, f32[384,16]{0,1:T(8,128)S(1)}, u32[]{:S(2)}, u32[]{:S(2)}) collective-permute-start(f32[384,16]{0,1:T(8,128)S(1)} %get-tuple-element.14), channel_id=1, source_target_pairs={{0,7},{1,8},{2,9},{3,10},{4,11},{5,12},{6,13},{7,14},{8,15},{9,16}... | collective-permute-start | bytes 73736
  444.9 10.8 %collective-permute-start.10 = (f32[384,16]{0,1:T(8,128)S(1)}, f32[384,16]{0,1:T(8,128)S(1)}, u32[]{:S(2)}, u32[]{:S(2)}) collective-permute-start(f32[384,16]{0,1:T(8,128)S(1)} %get-tuple-element.12), channel_id=1, source_target_pairs={{0,3},{1,4},{2,5},{3,6},{4,7},{5,8},{6,9},{7,10},{8,11},{9,12},{10... | collective-permute-start | bytes 73736
  446.7 10.5 %collective-permute-start.11 = (f32[384,16]{0,1:T(8,128)S(1)}, f32[384,16]{0,1:T(8,128)S(1)}, u32[]{:S(2)}, u32[]{:S(2)}) collective-permute-start(f32[384,16]{0,1:T(8,128)S(1)} %get-tuple-element.12), channel_id=1, source_target_pairs={{0,4},{1,5},{2,6},{3,7},{4,8},{5,9},{6,10},{7,11},{8,12},{9,13},{1... | collective-permute-start | bytes 73736
  449.4 11.4 %collective-permute-start.12 = (f32[384,16]{0,1:T(8,128)S(1)}, f32[384,16]{0,1:T(8,128)S(1)}, u32[]{:S(2)}, u32[]{:S(2)}) collective-permute-start(f32[384,16]{0,1:T(8,128)S(1)} %get-tuple-element.12), channel_id=1, source_target_pairs={{0,5},{1,6},{2,7},{3,8},{4,9},{5,10},{6,11},{7,12},{8,13},{9,14},{... | collective-permute-start | bytes 73736
  451.6 14.1 %collective-permute-start.13 = (f32[384,16]{0,1:T(8,128)S(1)}, f32[384,16]{0,1:T(8,128)S(1)}, u32[]{:S(2)}, u32[]{:S(2)}) collective-permute-start(f32[384,16]{0,1:T(8,128)S(1)} %get-tuple-element.12), channel_id=1, source_target_pairs={{0,6},{1,7},{2,8},{3,9},{4,10},{5,11},{6,12},{7,13},{8,14},{9,15},... | collective-permute-start | bytes 73736
  454.4 14.0 %collective-permute-start.14 = (f32[384,16]{0,1:T(8,128)S(1)}, f32[384,16]{0,1:T(8,128)S(1)}, u32[]{:S(2)}, u32[]{:S(2)}) collective-permute-start(f32[384,16]{0,1:T(8,128)S(1)} %get-tuple-element.12), channel_id=1, source_target_pairs={{0,7},{1,8},{2,9},{3,10},{4,11},{5,12},{6,13},{7,14},{8,15},{9,16}... | collective-permute-start | bytes 73736
  455.7 14.6 %collective-permute-start.8 = (f32[384,16]{0,1:T(8,128)S(1)}, f32[384,16]{0,1:T(8,128)S(1)}, u32[]{:S(2)}, u32[]{:S(2)}) collective-permute-start(f32[384,16]{0,1:T(8,128)S(1)} %get-tuple-element.12), channel_id=1, source_target_pairs={{0,1},{1,2},{2,3},{3,4},{4,5},{5,6},{6,7},{7,8},{8,9},{9,10},{10,1... | collective-permute-start | bytes 73736
  457.2 16.5 %collective-permute-start.9 = (f32[384,16]{0,1:T(8,128)S(1)}, f32[384,16]{0,1:T(8,128)}, u32[]{:S(2)}, u32[]{:S(2)}) collective-permute-start(f32[384,16]{0,1:T(8,128)S(1)} %get-tuple-element.12), channel_id=1, source_target_pairs={{0,2},{1,3},{2,4},{3,5},{4,6},{5,7},{6,8},{7,9},{8,10},{9,11},{10,... | collective-permute-start | bytes 73736
  460.8 17.1 %collective-permute-start.23 = (f32[384,36]{0,1:T(8,128)S(1)}, f32[384,36]{0,1:T(8,128)S(1)}, u32[]{:S(2)}, u32[]{:S(2)}) collective-permute-start(f32[384,36]{0,1:T(8,128)S(1)} %slice.32), channel_id=1, source_target_pairs={{0,8},{1,9},{2,10},{3,11},{4,12},{5,13},{6,14},{7,15},{8,16},{9,17... | collective-permute-start | bytes 165896
  462.1 44.4 %copy-start.1 = (bf16[384,1152]{1,0:T(8,128)(2,1)S(1)}, bf16[384,1152]{1,0:T(8,128)(2,1)}, u32[]{:S(2)}) copy-start(bf16[384,1152]{1,0:T(8,128)(2,1)} %param.10) | copy-start | bytes 2654212
  465.7 14.2 %collective-permute-start.16 = (f32[384,48]{0,1:T(8,128)S(1)}, f32[384,48]{0,1:T(8,128)S(1)}, u32[]{:S(2)}, u32[]{:S(2)}) collective-permute-start(f32[384,48]{0,1:T(8,128)S(1)} %get-tuple-element.13), channel_id=1, source_target_pairs={{0,1},{1,2},{2,3},{3,4},{4,5},{5,6},{6,7},{7,8},{8,9},{9,10},{10,1... | collective-permute-start | bytes 221192
  468.5 13.8 %collective-permute-start.17 = (f32[384,48]{0,1:T(8,128)S(1)}, f32[384,48]{0,1:T(8,128)S(1)}, u32[]{:S(2)}, u32[]{:S(2)}) collective-permute-start(f32[384,48]{0,1:T(8,128)S(1)} %get-tuple-element.13), channel_id=1, source_target_pairs={{0,2},{1,3},{2,4},{3,5},{4,6},{5,7},{6,8},{7,9},{8,10},{9,11},{10,... | collective-permute-start | bytes 221192
  470.3 13.5 %collective-permute-start.18 = (f32[384,48]{0,1:T(8,128)S(1)}, f32[384,48]{0,1:T(8,128)S(1)}, u32[]{:S(2)}, u32[]{:S(2)}) collective-permute-start(f32[384,48]{0,1:T(8,128)S(1)} %get-tuple-element.13), channel_id=1, source_target_pairs={{0,3},{1,4},{2,5},{3,6},{4,7},{5,8},{6,9},{7,10},{8,11},{9,12},{10... | collective-permute-start | bytes 221192
  473.7 11.5 %collective-permute-start.19 = (f32[384,48]{0,1:T(8,128)S(1)}, f32[384,48]{0,1:T(8,128)S(1)}, u32[]{:S(2)}, u32[]{:S(2)}) collective-permute-start(f32[384,48]{0,1:T(8,128)S(1)} %get-tuple-element.13), channel_id=1, source_target_pairs={{0,4},{1,5},{2,6},{3,7},{4,8},{5,9},{6,10},{7,11},{8,12},{9,13},{1... | collective-permute-start | bytes 221192
  478.0 9.5 %collective-permute-start.20 = (f32[384,48]{0,1:T(8,128)S(1)}, f32[384,48]{0,1:T(8,128)S(1)}, u32[]{:S(2)}, u32[]{:S(2)}) collective-permute-start(f32[384,48]{0,1:T(8,128)S(1)} %get-tuple-element.13), channel_id=1, source_target_pairs={{0,5},{1,6},{2,7},{3,8},{4,9},{5,10},{6,11},{7,12},{8,13},{9,14},{... | collective-permute-start | bytes 221192
  479.9 9.9 %collective-permute-start.21 = (f32[384,48]{0,1:T(8,128)S(1)}, f32[384,48]{0,1:T(8,128)S(1)}, u32[]{:S(2)}, u32[]{:S(2)}) collective-permute-start(f32[384,48]{0,1:T(8,128)S(1)} %get-tuple-element.13), channel_id=1, source_target_pairs={{0,6},{1,7},{2,8},{3,9},{4,10},{5,11},{6,12},{7,13},{8,14},{9,15},... | collective-permute-start | bytes 221192
  482.3 10.5 %collective-permute-start.22 = (f32[384,48]{0,1:T(8,128)S(1)}, f32[384,48]{0,1:T(8,128)S(1)}, u32[]{:S(2)}, u32[]{:S(2)}) collective-permute-start(f32[384,48]{0,1:T(8,128)S(1)} %get-tuple-element.13), channel_id=1, source_target_pairs={{0,7},{1,8},{2,9},{3,10},{4,11},{5,12},{6,13},{7,14},{8,15},{9,16}... | collective-permute-start | bytes 221192
  483.8 14.4 %collective-permute-start = (f32[384,48]{0,1:T(8,128)S(1)}, f32[384,48]{0,1:T(8,128)S(1)}, u32[]{:S(2)}, u32[]{:S(2)}) collective-permute-start(f32[384,48]{0,1:T(8,128)S(1)} %get-tuple-element.11), channel_id=1, source_target_pairs={{0,1},{1,2},{2,3},{3,4},{4,5},{5,6},{6,7},{7,8},{8,9},{9,10},{10,1... | collective-permute-start | bytes 221192
  485.2 16.1 %collective-permute-start.1 = (f32[384,48]{0,1:T(8,128)S(1)}, f32[384,48]{0,1:T(8,128)S(1)}, u32[]{:S(2)}, u32[]{:S(2)}) collective-permute-start(f32[384,48]{0,1:T(8,128)S(1)} %get-tuple-element.11), channel_id=1, source_target_pairs={{0,2},{1,3},{2,4},{3,5},{4,6},{5,7},{6,8},{7,9},{8,10},{9,11},{10,... | collective-permute-start | bytes 221192
  487.5 9.2 %collective-permute-start.7 = (f32[384,36]{0,1:T(8,128)S(1)}, f32[384,36]{0,1:T(8,128)S(1)}, u32[]{:S(2)}, u32[]{:S(2)}) collective-permute-start(f32[384,36]{0,1:T(8,128)S(1)} %slice.30), channel_id=1, source_target_pairs={{0,8},{1,9},{2,10},{3,11},{4,12},{5,13},{6,14},{7,15},{8,16},{9,17... | collective-permute-start | bytes 165896
  489.8 13.5 %collective-permute-start.2 = (f32[384,48]{0,1:T(8,128)S(1)}, f32[384,48]{0,1:T(8,128)S(1)}, u32[]{:S(2)}, u32[]{:S(2)}) collective-permute-start(f32[384,48]{0,1:T(8,128)S(1)} %get-tuple-element.11), channel_id=1, source_target_pairs={{0,3},{1,4},{2,5},{3,6},{4,7},{5,8},{6,9},{7,10},{8,11},{9,12},{10... | collective-permute-start | bytes 221192
  492.8 10.5 %collective-permute-start.3 = (f32[384,48]{0,1:T(8,128)S(1)}, f32[384,48]{0,1:T(8,128)S(1)}, u32[]{:S(2)}, u32[]{:S(2)}) collective-permute-start(f32[384,48]{0,1:T(8,128)S(1)} %get-tuple-element.11), channel_id=1, source_target_pairs={{0,4},{1,5},{2,6},{3,7},{4,8},{5,9},{6,10},{7,11},{8,12},{9,13},{1... | collective-permute-start | bytes 221192
  496.7 6.6 %collective-permute-start.4 = (f32[384,48]{0,1:T(8,128)S(1)}, f32[384,48]{0,1:T(8,128)S(1)}, u32[]{:S(2)}, u32[]{:S(2)}) collective-permute-start(f32[384,48]{0,1:T(8,128)S(1)} %get-tuple-element.11), channel_id=1, source_target_pairs={{0,5},{1,6},{2,7},{3,8},{4,9},{5,10},{6,11},{7,12},{8,13},{9,14},{... | collective-permute-start | bytes 221192
  498.2 5.1 %collective-permute-start.5 = (f32[384,48]{0,1:T(8,128)S(1)}, f32[384,48]{0,1:T(8,128)S(1)}, u32[]{:S(2)}, u32[]{:S(2)}) collective-permute-start(f32[384,48]{0,1:T(8,128)S(1)} %get-tuple-element.11), channel_id=1, source_target_pairs={{0,6},{1,7},{2,8},{3,9},{4,10},{5,11},{6,12},{7,13},{8,14},{9,15},... | collective-permute-start | bytes 221192
  501.3 3.3 collective-permute-start.6
  (16 other events, 53.5 us)
where the time goes:
time: 513 us; the launch traced here: 507 us
  matrix products  168 us (33%)
  starting transfers between devices  85.9 us (17%)
  blocking collectives  82.3 us (16%)
  local copies, waits for them, and re-layouts  75.3 us (15%)
  waiting for transfers between devices  59.1 us (12%)
  other arithmetic  34.5 us (7%)
    dot_general x19, matrix products, product(): return jnp.einsum(pattern, left, right, preferred_element_type=jnp.float32)  141 us
    unnamed x1, blocking collectives  82.3 us
    unnamed x32, starting transfers between devices  70.1 us
    all_to_all x1, waiting for transfers between devices, on_device(): lax.all_to_all(stream, 'seq', split_axis=2, concat_axis=1, tiled=True)  33.9 us
    all_to_all x1, waiting for transfers between devices, on_device(): lax.all_to_all(branch_t, 'seq', split_axis=1, concat_axis=2, tiled=True)  20.9 us
    unnamed x71, local copies, waits for them, and re-layouts  18 us
    sub x1, matrix products, attend_block(): probs = jax.nn.softmax(scores, axis=-1).astype(jnp.bfloat16)  14.3 us
    convert_element_type x2, other arithmetic, attend_block(): probs = jax.nn.softmax(scores, axis=-1).astype(jnp.bfloat16)  13 us
  transfers between devices with their start and end apart: 35, of which 4 were waited for; matrix products, arithmetic and copies ran while one was open for 15% of the time, Pallas kernels for 0%

commit v1 on v0

v1 whole, which is shorter than its diff:
```python
import functools
import math

import jax
import jax.numpy as jnp
from jax import lax
from jax.experimental import pallas as pl
from jax.experimental.pallas import tpu as pltpu
from jax.sharding import PartitionSpec as P

HEADS = 6
PAIR = 128
MESH = pl.DeviceIdType.MESH
BF16 = jnp.bfloat16
F32 = jnp.float32
VMEM_LIMIT = 56 * 1024 * 1024


def nn(left, right):
    return lax.dot_general(left, right, (((1,), (0,)), ((), ())), preferred_element_type=F32)


def nt(left, right):
    return lax.dot_general(left, right, (((1,), (1,)), ((), ())), preferred_element_type=F32)


def tn(left, right):
    return lax.dot_general(left, right, (((0,), (0,)), ((), ())), preferred_element_type=F32)


def normalize(values):
    average = jnp.mean(values, -1, keepdims=True)
    centered = values - average
    spread = jnp.mean(centered * centered, -1, keepdims=True)
    inverse = lax.rsqrt(spread + 1e-06)
    return (centered * inverse, inverse)


def normalize_back(scaled, inverse, upstream):
    return inverse * (
        upstream
        - jnp.mean(upstream, -1, keepdims=True)
        - scaled * jnp.mean(upstream * scaled, -1, keepdims=True)
    )


def two_heads(rows):
    first = lax.broadcasted_iota(jnp.int32, rows.shape, 1) < PAIR // 2
    none = jnp.zeros_like(rows)
    return jnp.concatenate([jnp.where(first, rows, none), jnp.where(first, none, rows)], 0)


def own_head(both):
    group = both.shape[1] // 2
    first = lax.broadcasted_iota(jnp.int32, (PAIR, group), 0) < PAIR // 2
    return jnp.where(first, both[:, :group], both[:, group:]).T


def pair_forward(queries, keys, values):
    scores = nt(keys, two_heads(queries))
    factor = math.log2(math.e) * (PAIR // 2) ** (-0.5)
    powers = jnp.exp2((scores - jnp.max(scores, 0, keepdims=True)) * factor)
    probs = (powers * (1.0 / jnp.sum(powers, 0, keepdims=True))).astype(BF16)
    return probs, own_head(tn(values, probs)).astype(BF16)


def pair_backward(queries, keys, values, upstream, probs):
    upstream = two_heads(upstream)
    prob_grad = nt(values, upstream)
    weights = probs.astype(F32)
    total = jnp.sum(weights * prob_grad, 0, keepdims=True)
    factor = (PAIR // 2) ** (-0.5)
    score_grad = (weights * ((prob_grad - total) * factor)).astype(BF16)
    query_grad = own_head(tn(keys, score_grad)).astype(BF16)
    key_grad = nn(score_grad, two_heads(queries)).astype(BF16)
    value_grad = nn(probs, upstream).astype(BF16)
    return query_grad, key_grad, value_grad


def three(combined, pair, width):
    return [combined[..., k * width + pair * PAIR : k * width + (pair + 1) * PAIR] for k in range(3)]


def offset(step, n):
    return (step % 2) * (n // 2) + step // 2


def greet(me, n):
    barrier = pltpu.get_barrier_semaphore()

    def say(step, carry):
        pl.semaphore_signal(
            barrier, inc=1, device_id={"seq": lax.rem(me + step, n)}, device_id_type=MESH
        )
        return carry

    lax.fori_loop(1, n, say, 0)
    pl.semaphore_wait(barrier, n - 1)


def each_other(n, body):
    def run(step, carry):
        body(offset(step, n))
        return carry

    lax.fori_loop(1, n, run, 0)


def forward_kernel(
    n, x_ref, wqkv_ref, wo_ref, cot_ref,
    probs_ref, combined_ref, attended_ref, stream_out, cot_out,
    rows, send, recv, cot_send, cot_recv, local,
):
    frame = pl.program_id(0)
    frames = pl.num_programs(0)
    me = lax.axis_index("seq")
    width = x_ref.shape[-1]

    def cot_copy(k):
        to = lax.rem(me + k, n)
        return pltpu.make_async_remote_copy(
            src_ref=cot_ref.at[:, to], dst_ref=cot_out.at[me],
            send_sem=cot_send.at[k], recv_sem=cot_recv.at[k],
            device_id={"seq": to}, device_id_type=MESH,
        )

    def frame_copy(k):
        to = lax.rem(me + k, n)
        return pltpu.make_async_remote_copy(
            src_ref=rows.at[frame, to], dst_ref=stream_out.at[me, frame],
            send_sem=send.at[k], recv_sem=recv.at[k],
            device_id={"seq": to}, device_id_type=MESH,
        )

    def stream_copy(k):
        to = lax.rem(me + k, n)
        return pltpu.make_async_remote_copy(
            src_ref=rows.at[:, to], dst_ref=stream_out.at[me],
            send_sem=send.at[k], recv_sem=recv.at[k],
            device_id={"seq": to}, device_id_type=MESH,
        )

    own_cot = pltpu.make_async_copy(cot_ref.at[:, me], cot_out.at[me], local.at[0])
    own_stream = pltpu.make_async_copy(rows.at[:, me], stream_out.at[me], local.at[1])

    @pl.when(frame == 0)
    def _():
        greet(me, n)
        each_other(n, lambda k: cot_copy(k).start())
        own_cot.start()

    x = x_ref[0].astype(F32)
    scaled, _ = normalize(x)
    combined = nn(scaled.astype(BF16), wqkv_ref[...]).astype(BF16)
    combined_ref[0] = combined
    heads = []
    for pair in range(width // PAIR):
        probs, out = pair_forward(*three(combined, pair, width))
        probs_ref[0, pair] = probs
        heads.append(out)
    attended = jnp.concatenate(heads, 1)
    attended_ref[0] = attended
    stream = (x + nn(attended, wo_ref[...])).astype(BF16)
    rows[frame] = stream.reshape(rows.shape[1:])
    each_other(n, lambda k: frame_copy(k).start())

    @pl.when(frame == frames - 1)
    def _():
        own_stream.start()
        own_cot.wait()
        own_stream.wait()

        def finish(k):
            cot_copy(k).wait()
            stream_copy(k).wait()

        each_other(n, finish)


def temporal_kernel(
    n, stream_ref, cot_ref, wqkv_ref, wo_ref,
    wqkv_grad_ref, wo_grad_ref, branch_out,
    stream_rows, cot_rows, rows, wqkv_sum, wo_sum, send, recv, local,
):
    me = lax.axis_index("seq")
    local_frames, patches, width = branch_out.shape[0], branch_out.shape[2], branch_out.shape[3]
    frames = n * local_frames
    together = min(4, patches)
    greet(me, n)
    lanes = width // PAIR
    for c in range(lanes):
        stream_rows[c] = stream_ref[:, c * PAIR : (c + 1) * PAIR].astype(F32)
        cot_rows[c] = cot_ref[:, c * PAIR : (c + 1) * PAIR].astype(F32)
    wqkv_sum[...] = jnp.zeros_like(wqkv_sum)
    wo_sum[...] = jnp.zeros_like(wo_sum)

    def group(number, carry):
        first = number * together
        spots = [pl.ds(first + i, frames, stride=patches) for i in range(together)]

        def gather(ref):
            return jnp.concatenate(
                [jnp.concatenate([ref[c, s, :] for s in spots], 0) for c in range(lanes)], 1
            )

        scaled, inverse = normalize(gather(stream_rows))
        normed = scaled.astype(BF16)
        cot = gather(cot_rows).astype(BF16)
        combined = nn(normed, wqkv_ref[...]).astype(BF16)
        upstream = nt(cot, wo_ref[...]).astype(BF16)
        outs, grads = [], []
        for i in range(together):
            part = slice(i * frames, (i + 1) * frames)
            out, grad = [], []
            for pair in range(width // PAIR):
                q, k, v = three(combined[part], pair, width)
                probs, attended = pair_forward(q, k, v)
                up = upstream[part, pair * PAIR : (pair + 1) * PAIR]
                out.append(attended)
                grad.append(pair_backward(q, k, v, up, probs))
            outs.append(jnp.concatenate(out, 1))
            grads.append(jnp.concatenate([g[j] for j in range(3) for g in grad], 1))
        attended = jnp.concatenate(outs, 0)
        combined_grad = jnp.concatenate(grads, 0)
        wo_sum[...] += tn(cot, attended)
        wqkv_sum[...] += tn(combined_grad, normed)
        branch = normalize_back(scaled, inverse, nt(combined_grad, wqkv_ref[...]))
        for i, s in enumerate(spots):
            for c in range(lanes):
                stream_rows[c, s, :] = branch[
                    i * frames : (i + 1) * frames, c * PAIR : (c + 1) * PAIR
                ]
        return carry

    lax.fori_loop(0, patches // together, group, 0)
    for c in range(lanes):
        part = stream_rows[c].astype(BF16)
        rows[:, :, :, c * PAIR : (c + 1) * PAIR] = part.reshape(rows.shape[:3] + (PAIR,))

    def copy(k):
        to = lax.rem(me + k, n)
        return pltpu.make_async_remote_copy(
            src_ref=rows.at[to], dst_ref=branch_out.at[:, me],
            send_sem=send.at[k], recv_sem=recv.at[k],
            device_id={"seq": to}, device_id_type=MESH,
        )

    each_other(n, lambda k: copy(k).start())
    own = pltpu.make_async_copy(rows.at[me], branch_out.at[:, me], local.at[0])
    own.start()
    scale = (lax.axis_size("dp") * frames * patches * n) ** (-0.5)
    wqkv_grad_ref[...] = (wqkv_sum[...] * scale).astype(BF16)
    wo_grad_ref[...] = (wo_sum[...] * scale).astype(BF16)
    own.wait()
    each_other(n, lambda k: copy(k).wait())


def backward_kernel(
    scale, x_ref, cot_ref, branch_ref, probs_ref, combined_ref, attended_ref, wqkv_ref, wo_ref,
    token_grad_ref, wqkv_grad_ref, wo_grad_ref, wqkv_sum, wo_sum,
):
    frame = pl.program_id(0)
    width = x_ref.shape[-1]

    @pl.when(frame == 0)
    def _():
        wqkv_sum[...] = jnp.zeros_like(wqkv_sum)
        wo_sum[...] = jnp.zeros_like(wo_sum)

    stream_grad = (cot_ref[0].astype(F32) + branch_ref[0].astype(F32)).astype(BF16)
    wo_sum[...] += tn(stream_grad, attended_ref[0])
    upstream = nt(stream_grad, wo_ref[...]).astype(BF16)
    combined = combined_ref[0]
    grads = []
    for pair in range(width // PAIR):
        q, k, v = three(combined, pair, width)
        up = upstream[:, pair * PAIR : (pair + 1) * PAIR]
        grads.append(pair_backward(q, k, v, up, probs_ref[0, pair]))
    combined_grad = jnp.concatenate([g[j] for j in range(3) for g in grads], 1)
    scaled, inverse = normalize(x_ref[0].astype(F32))
    wqkv_sum[...] += tn(combined_grad, scaled.astype(BF16))
    input_grad = nt(combined_grad, wqkv_ref[...])
    token_grad_ref[0] = (
        stream_grad.astype(F32) + normalize_back(scaled, inverse, input_grad)
    ).astype(BF16)

    @pl.when(frame == pl.num_programs(0) - 1)
    def _():
        wqkv_grad_ref[...] = (wqkv_sum[...] * scale).astype(BF16)
        wo_grad_ref[...] = (wo_sum[...] * scale).astype(BF16)


def scatter_sum(wqkv_grad, wo_grad, n):
    width = wqkv_grad.shape[1]
    mine = jnp.concatenate(
        [wqkv_grad.reshape(n, -1, width), wo_grad.reshape(n, -1, width)], 1
    )
    me = lax.axis_index("seq")
    bit = 1
    while bit < n:
        side = lax.rem(me // bit, 2)
        halves = mine.reshape((mine.shape[0] // 2, 2) + mine.shape[1:])
        keep = lax.dynamic_index_in_dim(halves, side, 1, keepdims=False)
        give = lax.dynamic_index_in_dim(halves, 1 - side, 1, keepdims=False).astype(BF16)
        pairs = [(i, i ^ bit) for i in range(n)]
        got = lax.ppermute(give, "seq", pairs)
        mine = keep.astype(F32) + got.astype(F32)
        bit *= 2
    mine = lax.psum(mine[0], "dp")
    split = wqkv_grad.shape[0] // n
    return mine[:split].T, mine[split:].T


def full(shape):
    return pl.BlockSpec(shape, lambda f: (0,) * len(shape))


def per_frame(shape):
    return pl.BlockSpec((1,) + shape, lambda f: (f,) + (0,) * len(shape))


def on_device(tokens, cotangent, wqkv_spatial, wo_spatial, wqkv_temporal, wo_temporal):
    clips, frames, count, width = tokens.shape
    n = lax.axis_size("seq")
    patches = count // n
    total = frames * clips
    pairs = width // PAIR
    x = tokens.reshape(total, count, width)
    cot = cotangent.reshape(total, count, width)
    anywhere = pl.BlockSpec(memory_space=pl.ANY)
    whole = pl.BlockSpec(memory_space=pltpu.VMEM)
    shape = jax.ShapeDtypeStruct
    dma = pltpu.SemaphoreType.DMA
    probs, combined, attended, stream_t, cot_t = pl.pallas_call(
        functools.partial(forward_kernel, n),
        grid=(total,),
        in_specs=[
            per_frame((count, width)), full(wqkv_spatial.shape), full(wo_spatial.shape), anywhere,
        ],
        out_specs=[
            per_frame((pairs, count, 2 * count)), per_frame((count, 3 * width)),
            per_frame((count, width)), anywhere, anywhere,
        ],
        out_shape=[
            shape((total, pairs, count, 2 * count), BF16),
            shape((total, count, 3 * width), BF16),
            shape((total, count, width), BF16),
            shape((n, total, patches, width), BF16),
            shape((n, total, patches, width), BF16),
        ],
        scratch_shapes=[
            pltpu.VMEM((total, n, patches, width), BF16),
            dma((n,)), dma((n,)), dma((n,)), dma((n,)), dma((2,)),
        ],
        compiler_params=pltpu.CompilerParams(
            collective_id=0, has_side_effects=True, vmem_limit_bytes=VMEM_LIMIT
        ),
        name="spatial_forward",
    )(x, wqkv_spatial, wo_spatial, cot.reshape(total, n, patches, width))

    tokens_t = n * total * patches
    wqkv_grad_t, wo_grad_t, branch = pl.pallas_call(
        functools.partial(temporal_kernel, n),
        in_specs=[whole] * 4,
        out_specs=[whole, whole, anywhere],
        out_shape=[
            shape((3 * width, width), BF16),
            shape((width, width), BF16),
            shape((total, n, patches, width), BF16),
        ],
        scratch_shapes=[
            pltpu.VMEM((width // PAIR, tokens_t, PAIR), F32),
            pltpu.VMEM((width // PAIR, tokens_t, PAIR), F32),
            pltpu.VMEM((n, total, patches, width), BF16),
            pltpu.VMEM((3 * width, width), F32),
            pltpu.VMEM((width, width), F32),
            dma((n,)), dma((n,)), dma((1,)),
        ],
        compiler_params=pltpu.CompilerParams(
            collective_id=1, has_side_effects=True, vmem_limit_bytes=VMEM_LIMIT
        ),
        name="temporal",
    )(
        stream_t.reshape(tokens_t, width), cot_t.reshape(tokens_t, width),
        wqkv_temporal, wo_temporal,
    )

    scale = (total * count * n * lax.axis_size("dp")) ** (-0.5)
    token_grad, wqkv_grad_s, wo_grad_s = pl.pallas_call(
        functools.partial(backward_kernel, scale),
        grid=(total,),
        in_specs=[
            per_frame((count, width)), per_frame((count, width)), per_frame((count, width)),
            per_frame((pairs, count, 2 * count)), per_frame((count, 3 * width)),
            per_frame((count, width)), full(wqkv_spatial.shape), full(wo_spatial.shape),
        ],
        out_specs=[
            per_frame((count, width)), full((3 * width, width)), full((width, width)),
        ],
        out_shape=[
            shape((total, count, width), BF16),
            shape((3 * width, width), BF16),
            shape((width, width), BF16),
        ],
        scratch_shapes=[pltpu.VMEM((3 * width, width), F32), pltpu.VMEM((width, width), F32)],
        compiler_params=pltpu.CompilerParams(vmem_limit_bytes=VMEM_LIMIT),
        cost_estimate=pl.CostEstimate(
            flops=20 * total * count * width * (width + count),
            bytes_accessed=2 * total * count * (pairs * 2 * count + 8 * width),
            transcendentals=0,
        ),
        name="spatial_backward",
    )(
        x, cot, branch.reshape(total, count, width), probs, combined, attended,
        wqkv_spatial, wo_spatial,
    )
    wqkv_t, wo_t = scatter_sum(wqkv_grad_t, wo_grad_t, n)
    wqkv_s, wo_s = scatter_sum(wqkv_grad_s, wo_grad_s, n)
    return (token_grad.reshape(tokens.shape), wqkv_s, wo_s, wqkv_t, wo_t)


def solution(mesh):
    in_specs = (P("dp", "seq", None, None), P("dp", "seq", None, None), P(), P(), P(), P())
    out_specs = (
        P("dp", "seq", None, None),
        P(None, "seq"),
        P(None, "seq"),
        P(None, "seq"),
        P(None, "seq"),
    )
    return jax.shard_map(
        on_device, mesh=mesh, in_specs=in_specs, out_specs=out_specs, check_vma=False
    )
```

time: 513 us -> 222 us (0.43); the launches traced: 507 us -> 222 us
  Pallas kernels: 0 us -> 183 us
  matrix products: 168 us -> 0 us
  blocking collectives: 82.3 us -> 0 us
  starting transfers between devices: 85.9 us -> 7.7 us
  local copies, waits for them, and re-layouts: 75.3 us -> 4.95 us
  waiting for transfers between devices: 59.1 us -> 22.1 us
  other arithmetic: 34.5 us -> 3.5 us
    pallas_call x0 -> x3, Pallas kernels: none -> 183 us  [the longest x1 82.1 us: on_device(): pl.pallas_call(functools.partial(forward_kernel, n), grid=(total,), in_sp...]
    dot_general x22 -> x0, matrix products: 154 us -> none  [the longest x19 141 us: product(): return jnp.einsum(pattern, left, right, preferred_element_type=jnp.float32)]
    unnamed x1 -> x0, blocking collectives: 82.3 us -> none
    unnamed x32 -> x0, starting transfers between devices: 70.1 us -> none
    all_to_all x3 -> x0, waiting for transfers between devices: 57.7 us -> none  [the longest x1 33.9 us: on_device(): lax.all_to_all(stream, 'seq', split_axis=2, concat_axis=1, tiled=True)]
    convert_element_type x10 -> x8, local copies, waits for them, and re-layouts: 40.2 us -> 0.22 us  [scatter_sum(): lax.dynamic_index_in_dim(halves, 1 - side, 1, keepdims=False).astype(BF16)]
    ppermute x0 -> x10, waiting for transfers between devices: none -> 22.1 us  [scatter_sum(): got = lax.ppermute(give, 'seq', pairs)]
    convert_element_type x8 -> x0, other arithmetic: 20.3 us -> none  [the longest x2 13 us: attend_block(): probs = jax.nn.softmax(scores, axis=-1).astype(jnp.bfloat16)]
  transfers between devices with their start and end apart: 35 -> 10, of which waited for: 4 -> 7; matrix products, arithmetic and copies ran while one was open for 15% -> 2% of each run, Pallas kernels for 0% -> 0%
where the time goes in v1:
time: 222 us
  Pallas kernels  183 us (82%)
  waiting for transfers between devices  22.1 us (10%)
  starting transfers between devices  7.7 us (3%)
  local copies, waits for them, and re-layouts  4.95 us (2%)
  other arithmetic  3.5 us (2%)
    pallas_call x1, Pallas kernels, on_device(): pl.pallas_call(functools.partial(forward_kernel, n), grid=(total,), in_sp...  82.1 us
    pallas_call x1, Pallas kernels, on_device(): pl.pallas_call(functools.partial(temporal_kernel, n), in_specs=[whole] *...  70.6 us
    pallas_call x1, Pallas kernels, on_device(): pl.pallas_call(functools.partial(backward_kernel, scale), grid=(total,),...  30.4 us
    ppermute x10, waiting for transfers between devices, scatter_sum(): got = lax.ppermute(give, 'seq', pairs)  22.1 us
    ppermute x10, starting transfers between devices, scatter_sum(): got = lax.ppermute(give, 'seq', pairs)  7.7 us
  transfers between devices with their start and end apart: 10, of which 7 were waited for; matrix products, arithmetic and copies ran while one was open for 2% of the time, Pallas kernels for 0%

profile of v1, /device:TPU:0, one launch (start us, length us, event | category | flops | bytes accessed | tf_op | source)
XLA Modules:
  0.0 222.2 jit_solution(17907163040743905658)
XLA Ops:
  0.6 82.1 %spatial_forward.1 = (bf16[4,3,512,1024]{3,2,1,0:T(8,128)(2,1)}, bf16[4,512,1152]{2,1,0:T(8,128)(2,1)}, bf16[4,512,384]{2,1,0:T(8,128)(2,1)}, bf16[32,4,16,384]{3,2,1,0:T(8,128)(2,1)}, bf16[32,4,16,384]{3,2,1,0:T(8,128)(2,1)}) custom-call(bf16[4,512,384]{2,1,0:T(8,128)(2,1)} %bitcast.83, bf16[384,1152]{1,0:T(8,128)(2,1)} %wqkv_ref.5, ...), custom_call_target="tpu_custom_call" | custom-call | tf_op jit(solution)/shard_map/spatial_forward/pallas_call | solution.py:334
  82.7 70.6 %temporal.1 = (bf16[1152,384]{1,0:T(8,128)(2,1)}, bf16[384,384]{1,0:T(8,128)(2,1)}, bf16[4,32,16,384]{3,2,1,0:T(8,128)(2,1)}) custom-call(bf16[2048,384]{1,0:T(8,128)(2,1)} %bitcast.87, bf16[2048,384]{1,0:T(8,128)(2,1)} %bitcast.88, bf16[384,1152]{1,0:T(8,128)(2,1)} %wqkv_ref.4, bf16[384,384]{1,0:T(8,128)(2,1)} %wo_ref.4), custom_call_target="tpu_custom_call" | custom-call | tf_op jit(solution)/shard_map/temporal/pallas_call | solution.py:362
  153.3 30.4 %spatial_backward.1 = (bf16[4,512,384]{2,1,0:T(8,128)(2,1)}, bf16[1152,384]{1,0:T(8,128)(2,1)}, bf16[384,384]{1,0:T(8,128)(2,1)}) custom-call(bf16[4,512,384]{2,1,0:T(8,128)(2,1)} %bitcast.84, bf16[4,512,384]{2,1,0:T(8,128)(2,1)} %bitcast.86, bf16[4,512,384]{2,1,0:T(8,128)(2,1)} %bitcast.93, bf16[4,3,512,1024]{3,2,1,0:T(8,128)(2,1)} %get-tuple-element.19.probs_ref, ...), custom_call_target="tpu_custom_call" | custom-call | flops 14092861440 | bytes 25165824 | tf_op jit(solution)/shard_map/spatial_backward/pallas_call | solution.py:389
  183.8 0.0 copy-start.2
  183.8 1.3 concatenate.16
  185.1 0.0 copy-done.2
  185.1 0.0 copy-start
  185.1 0.1 concatenate.17
  185.2 0.9 fusion.5
  186.1 0.0 copy-start.1
  186.1 0.2 collective-permute-start
  186.3 0.1 copy-done
  186.4 0.2 concatenate.19
  186.5 0.6 copy-done.1
  187.1 0.1 concatenate.20
  187.2 0.9 fusion.1
  188.1 0.2 collective-permute-start.5
  188.3 0.1 collective-permute-done
  188.4 1.2 convert_add_fusion.1
  189.7 2.2 collective-permute-start.1
  191.9 0.0 collective-permute-done.5
  191.9 0.2 convert_add_fusion
  192.2 0.6 collective-permute-start.6
  192.7 7.0 %collective-permute-done.1 = bf16[8,48,384]{2,1,0:T(8,128)(2,1)S(1)} collective-permute-done((bf16[8,48,384]{2,1,0:T(8,128)(2,1)S(1)}, bf16[8,48,384]{2,1,0:T(8,128)(2,1)S(1)}, u32[]{:S(2)}, u32[]{:S(2)}) %collective-permute-start.1) | collective-permute-done | bytes 294944 | tf_op jit(solution)/shard_map/ppermute | solution.py:306
  199.7 0.1 bitcast_add_fusion.1
  199.8 1.3 collective-permute-start.2
  201.1 4.6 %collective-permute-done.6 = bf16[8,48,384]{2,1,0:T(8,128)(2,1)S(1)} collective-permute-done((bf16[8,48,384]{2,1,0:T(8,128)(2,1)S(1)}, bf16[8,48,384]{2,1,0:T(8,128)(2,1)S(1)}, u32[]{:S(2)}, u32[]{:S(2)}) %collective-permute-start.6) | collective-permute-done | bytes 294944 | tf_op jit(solution)/shard_map/ppermute | solution.py:306
  205.7 0.1 bitcast_add_fusion
  205.8 1.0 collective-permute-start.7
  206.8 0.0 collective-permute-done.2
  206.9 0.4 collective-permute-start.3
  207.3 4.1 %collective-permute-done.7 = bf16[4,48,384]{2,1,0:T(8,128)(2,1)S(1)} collective-permute-done((bf16[4,48,384]{2,1,0:T(8,128)(2,1)S(1)}, bf16[4,48,384]{2,1,0:T(8,128)(2,1)S(1)}, u32[]{:S(2)}, u32[]{:S(2)}) %collective-permute-start.7) | collective-permute-done | bytes 147488 | tf_op jit(solution)/shard_map/ppermute | solution.py:306
  211.5 0.1 collective-permute-start.8
  211.6 0.0 collective-permute-done.3
  211.7 1.6 collective-permute-start.4
  213.3 2.7 %collective-permute-done.8 = bf16[2,48,384]{2,1,0:T(8,128)(2,1)S(1)} collective-permute-done((bf16[2,48,384]{2,1,0:T(8,128)(2,1)S(1)}, bf16[2,48,384]{2,1,0:T(8,128)(2,1)S(1)}, u32[]{:S(2)}, u32[]{:S(2)}) %collective-permute-start.8) | collective-permute-done | bytes 73760 | tf_op jit(solution)/shard_map/ppermute | solution.py:306
  216.0 0.1 collective-permute-start.9
  216.1 0.5 collective-permute-done.4
  216.6 0.6 slice_bitcast_fusion.1
  217.2 0.6 slice_bitcast_fusion.3
  217.8 3.1 %collective-permute-done.9 = bf16[1,48,384]{2,1,0:T(8,128)(2,1)S(1)} collective-permute-done((bf16[1,48,384]{2,1,0:T(8,128)(2,1)S(1)}, bf16[1,48,384]{2,1,0:T(8,128)(2,1)S(1)}, u32[]{:S(2)}, u32[]{:S(2)}) %collective-permute-start.9) | collective-permute-done | bytes 36896 | tf_op jit(solution)/shard_map/ppermute | solution.py:306
  220.9 0.6 slice_bitcast_fusion
  221.5 0.6 slice_bitcast_fusion.2
  (14 shorter events, 0.3 us)
Async XLA Ops:
  183.8 1.3 copy-start.2
  185.1 1.3 copy-start
  186.1 1.0 copy-start.1
  186.1 2.3 %collective-permute-start = (bf16[16,48,384]{2,1,0:T(8,128)(2,1)}, bf16[16,48,384]{2,1,0:T(8,128)(2,1)}, u32[]{:S(2)}, u32[]{:S(2)}) collective-permute-start(bf16[16,48,384]{2,1,0:T(8,128)(2,1)} %fusion.5), channel_id=1, source_target_pairs={{0,1},{1,0},{2,3},{3,2},{4,5},{5,4},{6,7},{7,6},{8,9},{9,8},{10,11... | collective-permute-start | bytes 1769480 | tf_op jit(solution)/shard_map/ppermute | solution.py:306
  188.1 3.8 %collective-permute-start.5 = (bf16[16,48,384]{2,1,0:T(8,128)(2,1)}, bf16[16,48,384]{2,1,0:T(8,128)(2,1)S(1)}, u32[]{:S(2)}, u32[]{:S(2)}) collective-permute-start(bf16[16,48,384]{2,1,0:T(8,128)(2,1)} %fusion.1), channel_id=1, source_target_pairs={{0,1},{1,0},{2,3},{3,2},{4,5},{5,4},{6,7},{7,6},{8,9},{9,8},{10,11... | collective-permute-start | bytes 1769480 | tf_op jit(solution)/shard_map/ppermute | solution.py:306
  189.7 10.0 %collective-permute-start.1 = (bf16[8,48,384]{2,1,0:T(8,128)(2,1)S(1)}, bf16[8,48,384]{2,1,0:T(8,128)(2,1)S(1)}, u32[]{:S(2)}, u32[]{:S(2)}) collective-permute-start(bf16[8,48,384]{2,1,0:T(8,128)(2,1)S(1)} %fusion.8), channel_id=1, source_target_pairs={{0,2},{1,3},{2,0},{3,1},{4,6},{5,7},{6,4},{7,5},{8,10},{9,11},{10,... | collective-permute-start | bytes 884744 | tf_op jit(solution)/shard_map/ppermute | solution.py:306
  192.2 13.6 %collective-permute-start.6 = (bf16[8,48,384]{2,1,0:T(8,128)(2,1)S(1)}, bf16[8,48,384]{2,1,0:T(8,128)(2,1)S(1)}, u32[]{:S(2)}, u32[]{:S(2)}) collective-permute-start(bf16[8,48,384]{2,1,0:T(8,128)(2,1)S(1)} %fusion.9), channel_id=1, source_target_pairs={{0,2},{1,3},{2,0},{3,1},{4,6},{5,7},{6,4},{7,5},{8,10},{9,11},{10,... | collective-permute-start | bytes 884744 | tf_op jit(solution)/shard_map/ppermute | solution.py:306
  199.8 7.1 %collective-permute-start.2 = (bf16[4,48,384]{2,1,0:T(8,128)(2,1)S(1)}, bf16[4,48,384]{2,1,0:T(8,128)(2,1)S(1)}, u32[]{:S(2)}, u32[]{:S(2)}) collective-permute-start(bf16[4,48,384]{2,1,0:T(8,128)(2,1)S(1)} %fusion.10), channel_id=1, source_target_pairs={{0,4},{1,5},{2,6},{3,7},{4,0},{5,1},{6,2},{7,3},{8,12},{9,13},{10,... | collective-permute-start | bytes 442376 | tf_op jit(solution)/shard_map/ppermute | solution.py:306
  205.8 5.6 %collective-permute-start.7 = (bf16[4,48,384]{2,1,0:T(8,128)(2,1)S(1)}, bf16[4,48,384]{2,1,0:T(8,128)(2,1)S(1)}, u32[]{:S(2)}, u32[]{:S(2)}) collective-permute-start(bf16[4,48,384]{2,1,0:T(8,128)(2,1)S(1)} %fusion.11), channel_id=1, source_target_pairs={{0,4},{1,5},{2,6},{3,7},{4,0},{5,1},{6,2},{7,3},{8,12},{9,13},{10,... | collective-permute-start | bytes 442376 | tf_op jit(solution)/shard_map/ppermute | solution.py:306
  206.9 4.7 %collective-permute-start.3 = (bf16[2,48,384]{2,1,0:T(8,128)(2,1)S(1)}, bf16[2,48,384]{2,1,0:T(8,128)(2,1)S(1)}, u32[]{:S(2)}, u32[]{:S(2)}) collective-permute-start(bf16[2,48,384]{2,1,0:T(8,128)(2,1)S(1)} %fusion.12), channel_id=1, source_target_pairs={{0,8},{1,9},{2,10},{3,11},{4,12},{5,13},{6,14},{7,15},{8,0},{9,1},... | collective-permute-start | bytes 221192 | tf_op jit(solution)/shard_map/ppermute | solution.py:306
  211.5 4.4 %collective-permute-start.8 = (bf16[2,48,384]{2,1,0:T(8,128)(2,1)S(1)}, bf16[2,48,384]{2,1,0:T(8,128)(2,1)S(1)}, u32[]{:S(2)}, u32[]{:S(2)}) collective-permute-start(bf16[2,48,384]{2,1,0:T(8,128)(2,1)S(1)} %fusion.13), channel_id=1, source_target_pairs={{0,8},{1,9},{2,10},{3,11},{4,12},{5,13},{6,14},{7,15},{8,0},{9,1},... | collective-permute-start | bytes 221192 | tf_op jit(solution)/shard_map/ppermute | solution.py:306
  211.7 4.9 %collective-permute-start.4 = (bf16[1,48,384]{2,1,0:T(8,128)(2,1)S(1)}, bf16[1,48,384]{2,1,0:T(8,128)(2,1)S(1)}, u32[]{:S(2)}, u32[]{:S(2)}) collective-permute-start(bf16[1,48,384]{2,1,0:T(8,128)(2,1)S(1)} %dynamic-slice_convert_fusion.5), channel_id=1, source_target_pairs={{0,16},{1,17},{2,18},{3,19},{4,20},{5,21},{6,22},{7,23},{8,24},{9,... | collective-permute-start | bytes 110600 | tf_op jit(solution)/shard_map/ppermute | solution.py:306
  216.0 4.9 %collective-permute-start.9 = (bf16[1,48,384]{2,1,0:T(8,128)(2,1)S(1)}, bf16[1,48,384]{2,1,0:T(8,128)(2,1)S(1)}, u32[]{:S(2)}, u32[]{:S(2)}) collective-permute-start(bf16[1,48,384]{2,1,0:T(8,128)(2,1)S(1)} %dynamic-slice_convert_fusion.4), channel_id=1, source_target_pairs={{0,16},{1,17},{2,18},{3,19},{4,20},{5,21},{6,22},{7,23},{8,24},{9,... | collective-permute-start | bytes 110600 | tf_op jit(solution)/shard_map/ppermute | solution.py:306

commit v2 on v1

v2 whole, which is shorter than its diff:
```python
import functools
import math

import jax
import jax.numpy as jnp
from jax import lax
from jax.experimental import pallas as pl
from jax.experimental.pallas import tpu as pltpu
from jax.sharding import PartitionSpec as P

HEADS = 6
PAIR = 128
MESH = pl.DeviceIdType.MESH
BF16 = jnp.bfloat16
F32 = jnp.float32
VMEM_LIMIT = 60 * 1024 * 1024


def nn(left, right):
    return lax.dot_general(left, right, (((1,), (0,)), ((), ())), preferred_element_type=F32)


def nt(left, right):
    return lax.dot_general(left, right, (((1,), (1,)), ((), ())), preferred_element_type=F32)


def tn(left, right):
    return lax.dot_general(left, right, (((0,), (0,)), ((), ())), preferred_element_type=F32)


def normalize(values):
    average = jnp.mean(values, -1, keepdims=True)
    centered = values - average
    spread = jnp.mean(centered * centered, -1, keepdims=True)
    inverse = lax.rsqrt(spread + 1e-06)
    return (centered * inverse, inverse)


def normalize_back(scaled, inverse, upstream):
    return inverse * (
        upstream
        - jnp.mean(upstream, -1, keepdims=True)
        - scaled * jnp.mean(upstream * scaled, -1, keepdims=True)
    )


def two_heads(rows):
    first = lax.broadcasted_iota(jnp.int32, rows.shape, 1) < PAIR // 2
    none = jnp.zeros_like(rows)
    return jnp.concatenate([jnp.where(first, rows, none), jnp.where(first, none, rows)], 0)


def own_head(both):
    group = both.shape[1] // 2
    first = lax.broadcasted_iota(jnp.int32, (PAIR, group), 0) < PAIR // 2
    return jnp.where(first, both[:, :group], both[:, group:]).T


def pair_forward(queries, keys, values):
    scores = nt(keys, two_heads(queries))
    factor = math.log2(math.e) * (PAIR // 2) ** (-0.5)
    powers = jnp.exp2((scores - jnp.max(scores, 0, keepdims=True)) * factor)
    probs = (powers * (1.0 / jnp.sum(powers, 0, keepdims=True))).astype(BF16)
    return probs, own_head(tn(values, probs)).astype(BF16)


def pair_backward(queries, keys, values, upstream, probs):
    upstream = two_heads(upstream)
    prob_grad = nt(values, upstream)
    weights = probs.astype(F32)
    total = jnp.sum(weights * prob_grad, 0, keepdims=True)
    factor = (PAIR // 2) ** (-0.5)
    score_grad = (weights * ((prob_grad - total) * factor)).astype(BF16)
    query_grad = own_head(tn(keys, score_grad)).astype(BF16)
    key_grad = nn(score_grad, two_heads(queries)).astype(BF16)
    value_grad = nn(probs, upstream).astype(BF16)
    return query_grad, key_grad, value_grad


def three(combined, pair, width):
    return [combined[..., k * width + pair * PAIR : k * width + (pair + 1) * PAIR] for k in range(3)]


def offset(step, n):
    return (step % 2) * (n // 2) + step // 2


def greet(me, n):
    barrier = pltpu.get_barrier_semaphore()

    def say(step, carry):
        pl.semaphore_signal(
            barrier, inc=1, device_id={"seq": lax.rem(me + step, n)}, device_id_type=MESH
        )
        return carry

    lax.fori_loop(1, n, say, 0)
    pl.semaphore_wait(barrier, n - 1)


def each_other(n, body):
    def run(step, carry):
        body(offset(step, n))
        return carry

    lax.fori_loop(1, n, run, 0)


def kernel(
    n, halves, x_ref, cot_ref, wqkv_s_ref, wo_s_ref, wqkv_t_ref, wo_t_ref,
    token_grad_ref, wqkv_grad_s_ref, wo_grad_s_ref, wqkv_grad_t_ref, wo_grad_t_ref,
    probs_s, combined_s, attended_s, cot_send, stream_send, branch_send,
    cot_recv, stream_recv, branch_recv, stream_rows, cot_rows, wqkv_sum, wo_sum,
    cot_sems, stream_sems, branch_sems,
):
    me = lax.axis_index("seq")
    frames, count, width = x_ref.shape
    lanes = width // PAIR
    span = cot_send.shape[2] // frames
    together = 2 if halves == 2 else 1
    steps = frames // together
    slab = together * span
    all_frames = n * frames
    scale = (lax.axis_size("dp") * all_frames * count) ** (-0.5)

    def slab_of(step):
        return slice(None) if steps == 1 else pl.ds(pl.multiple_of(step * slab, slab), slab)

    def put(ref, step, members):
        parts = [member.reshape(n, halves, span, width) for member in members]
        for half in range(halves):
            rows = [part[:, half] for part in parts]
            ref[half, :, slab_of(step), :] = jnp.concatenate(rows, 1).astype(BF16)

    def get(ref, step):
        parts = [ref[half, :, slab_of(step), :].astype(F32) for half in range(halves)]
        return [
            jnp.concatenate([part[:, i * span : (i + 1) * span] for part in parts], 1).reshape(
                count, width
            )
            for i in range(together)
        ]

    def half_copy(source, target, sems, half, k):
        to = lax.rem(me + k, n)
        return pltpu.make_async_remote_copy(
            src_ref=source.at[half, to], dst_ref=target.at[half, me],
            send_sem=sems.at[0, half, k], recv_sem=sems.at[1, half, k],
            device_id={"seq": to}, device_id_type=MESH,
        )

    def slab_copy(half, step, k):
        to = lax.rem(me + k, n)
        return pltpu.make_async_remote_copy(
            src_ref=branch_send.at[half, to, slab_of(step)],
            dst_ref=branch_recv.at[half, me, slab_of(step)],
            send_sem=branch_sems.at[0, half, step, k], recv_sem=branch_sems.at[1, half, step, k],
            device_id={"seq": to}, device_id_type=MESH,
        )

    def cot_copy(half, k):
        return half_copy(cot_send, cot_recv, cot_sems, half, k)

    def stream_copy(half, k):
        return half_copy(stream_send, stream_recv, stream_sems, half, k)

    for step in range(steps):
        members = range(step * together, (step + 1) * together)
        put(cot_send, step, [cot_ref[frame].astype(F32) for frame in members])
    greet(me, n)
    each_other(n, lambda k: cot_copy(0, k).start())

    def forward(step, carry):
        streams = []
        for i in range(together):
            frame = step * together + i
            x = x_ref[frame].astype(F32)
            scaled, _ = normalize(x)
            combined = nn(scaled.astype(BF16), wqkv_s_ref[...]).astype(BF16)
            combined_s[frame] = combined
            heads = []
            for pair in range(lanes):
                probs, out = pair_forward(*three(combined, pair, width))
                probs_s[frame, pair] = probs
                heads.append(out)
            attended = jnp.concatenate(heads, 1)
            attended_s[frame] = attended
            streams.append(x + nn(attended, wo_s_ref[...]))
        put(stream_send, step, streams)
        return carry

    lax.fori_loop(0, steps, forward, 0)
    each_other(n, lambda k: stream_copy(0, k).start())
    for half in range(1, halves):
        each_other(n, lambda k: cot_copy(half, k).start())
        each_other(n, lambda k: stream_copy(half, k).start())
    for half in range(halves):
        cot_recv[half, me] = cot_send[half, me]
        stream_recv[half, me] = stream_send[half, me]

    wqkv_sum[...] = jnp.zeros_like(wqkv_sum)
    wo_sum[...] = jnp.zeros_like(wo_sum)
    few = min(4, span)

    def temporal(number, carry):
        spots = [pl.ds(number * few + i, all_frames, stride=span) for i in range(few)]

        def gather(ref):
            return jnp.concatenate(
                [jnp.concatenate([ref[c, s, :] for s in spots], 0) for c in range(lanes)], 1
            )

        scaled, inverse = normalize(gather(stream_rows))
        normed = scaled.astype(BF16)
        cot = gather(cot_rows).astype(BF16)
        combined = nn(normed, wqkv_t_ref[...]).astype(BF16)
        upstream = nt(cot, wo_t_ref[...]).astype(BF16)
        outs, grads = [], []
        for i in range(few):
            part = slice(i * all_frames, (i + 1) * all_frames)
            out, grad = [], []
            for pair in range(lanes):
                q, k, v = three(combined[part], pair, width)
                probs, attended = pair_forward(q, k, v)
                up = upstream[part, pair * PAIR : (pair + 1) * PAIR]
                out.append(attended)
                grad.append(pair_backward(q, k, v, up, probs))
            outs.append(jnp.concatenate(out, 1))
            grads.append(jnp.concatenate([g[j] for j in range(3) for g in grad], 1))
        attended = jnp.concatenate(outs, 0)
        combined_grad = jnp.concatenate(grads, 0)
        wo_sum[...] += tn(cot, attended)
        wqkv_sum[...] += tn(combined_grad, normed)
        branch = normalize_back(scaled, inverse, nt(combined_grad, wqkv_t_ref[...]))
        for i, s in enumerate(spots):
            for c in range(lanes):
                stream_rows[c, s, :] = branch[
                    i * all_frames : (i + 1) * all_frames, c * PAIR : (c + 1) * PAIR
                ]
        return carry

    for half in range(halves):

        def arrive(k):
            cot_copy(half, k).wait_recv()
            stream_copy(half, k).wait_recv()

        each_other(n, arrive)
        for c in range(lanes):
            part = slice(c * PAIR, (c + 1) * PAIR)
            flat = stream_rows.shape[1:]
            stream_rows[c] = stream_recv[half, :, :, part].astype(F32).reshape(flat)
            cot_rows[c] = cot_recv[half, :, :, part].astype(F32).reshape(flat)
        lax.fori_loop(0, span // few, temporal, 0)
        for c in range(lanes):
            part = stream_rows[c].reshape(branch_send.shape[1:3] + (PAIR,)).astype(BF16)
            branch_send[half, :, :, c * PAIR : (c + 1) * PAIR] = part
        for step in range(steps):
            each_other(n, lambda k: slab_copy(half, step, k).start())
        branch_recv[half, me] = branch_send[half, me]

    wqkv_grad_t_ref[...] = (wqkv_sum[...] * scale).astype(BF16)
    wo_grad_t_ref[...] = (wo_sum[...] * scale).astype(BF16)
    wqkv_sum[...] = jnp.zeros_like(wqkv_sum)
    wo_sum[...] = jnp.zeros_like(wo_sum)

    def backward(step, carry):
        def arrive(k):
            for half in range(halves):
                slab_copy(half, step, k).wait_recv()

        each_other(n, arrive)
        for i, branch in enumerate(get(branch_recv, step)):
            frame = step * together + i
            stream_grad = (cot_ref[frame].astype(F32) + branch).astype(BF16)
            wo_sum[...] += tn(stream_grad, attended_s[frame])
            upstream = nt(stream_grad, wo_s_ref[...]).astype(BF16)
            combined = combined_s[frame]
            grads = []
            for pair in range(lanes):
                q, k, v = three(combined, pair, width)
                up = upstream[:, pair * PAIR : (pair + 1) * PAIR]
                grads.append(pair_backward(q, k, v, up, probs_s[frame, pair]))
            combined_grad = jnp.concatenate([g[j] for j in range(3) for g in grads], 1)
            scaled, inverse = normalize(x_ref[frame].astype(F32))
            wqkv_sum[...] += tn(combined_grad, scaled.astype(BF16))
            input_grad = nt(combined_grad, wqkv_s_ref[...])
            token_grad_ref[frame] = (
                stream_grad.astype(F32) + normalize_back(scaled, inverse, input_grad)
            ).astype(BF16)
        return carry

    lax.fori_loop(0, steps, backward, 0)
    wqkv_grad_s_ref[...] = (wqkv_sum[...] * scale).astype(BF16)
    wo_grad_s_ref[...] = (wo_sum[...] * scale).astype(BF16)

    def left(k):
        for half in range(halves):
            cot_copy(half, k).wait_send()
            stream_copy(half, k).wait_send()
            for step in range(steps):
                slab_copy(half, step, k).wait_send()

    each_other(n, left)


def scatter_sum(wqkv_grad, wo_grad, n):
    width = wqkv_grad.shape[1]
    mine = jnp.concatenate(
        [wqkv_grad.reshape(n, -1, width), wo_grad.reshape(n, -1, width)], 1
    )
    me = lax.axis_index("seq")
    bit = 1
    while bit < n:
        side = lax.rem(me // bit, 2)
        halves = mine.reshape((mine.shape[0] // 2, 2) + mine.shape[1:])
        keep = lax.dynamic_index_in_dim(halves, side, 1, keepdims=False)
        give = lax.dynamic_index_in_dim(halves, 1 - side, 1, keepdims=False).astype(BF16)
        pairs = [(i, i ^ bit) for i in range(n)]
        got = lax.ppermute(give, "seq", pairs)
        mine = keep.astype(F32) + got.astype(F32)
        bit *= 2
    mine = lax.psum(mine[0], "dp")
    split = wqkv_grad.shape[0] // n
    return mine[:split].T, mine[split:].T


def on_device(tokens, cotangent, wqkv_spatial, wo_spatial, wqkv_temporal, wo_temporal):
    clips, frames, count, width = tokens.shape
    n = lax.axis_size("seq")
    patches = count // n
    total = frames * clips
    pairs = width // PAIR
    halves = 2 if patches == 16 and total % 2 == 0 else 1
    span = patches // halves
    whole = pl.BlockSpec(memory_space=pltpu.VMEM)
    shape = jax.ShapeDtypeStruct
    sems = pltpu.SemaphoreType.DMA
    exchanged = pltpu.VMEM((halves, n, total * span, width), BF16)
    gathered = pltpu.VMEM((pairs, n * total * span, PAIR), F32)
    token_grad, wqkv_grad_s, wo_grad_s, wqkv_grad_t, wo_grad_t = pl.pallas_call(
        functools.partial(kernel, n, halves),
        in_specs=[whole] * 6,
        out_specs=[whole] * 5,
        out_shape=[shape((total, count, width), BF16)]
        + [shape((3 * width, width), BF16), shape((width, width), BF16)] * 2,
        scratch_shapes=[
            pltpu.VMEM((total, pairs, count, 2 * count), BF16),
            pltpu.VMEM((total, count, 3 * width), BF16),
            pltpu.VMEM((total, count, width), BF16),
        ]
        + [exchanged] * 6
        + [gathered] * 2
        + [
            pltpu.VMEM((3 * width, width), F32),
            pltpu.VMEM((width, width), F32),
            sems((2, halves, n)), sems((2, halves, n)),
            sems((2, halves, max(total // 2, 1), n)),
        ],
        compiler_params=pltpu.CompilerParams(
            collective_id=0, has_side_effects=True, vmem_limit_bytes=VMEM_LIMIT
        ),
        name="space_time_backward",
    )(
        tokens.reshape(total, count, width), cotangent.reshape(total, count, width),
        wqkv_spatial, wo_spatial, wqkv_temporal, wo_temporal,
    )
    wqkv_t, wo_t = scatter_sum(wqkv_grad_t, wo_grad_t, n)
    wqkv_s, wo_s = scatter_sum(wqkv_grad_s, wo_grad_s, n)
    return (token_grad.reshape(tokens.shape), wqkv_s, wo_s, wqkv_t, wo_t)


def solution(mesh):
    in_specs = (P("dp", "seq", None, None), P("dp", "seq", None, None), P(), P(), P(), P())
    out_specs = (
        P("dp", "seq", None, None),
        P(None, "seq"),
        P(None, "seq"),
        P(None, "seq"),
        P(None, "seq"),
    )
    return jax.shard_map(
        on_device, mesh=mesh, in_specs=in_specs, out_specs=out_specs, check_vma=False
    )
```

time: 222 us -> 184 us (0.83)
  Pallas kernels: 183 us -> 143 us
    pallas_call x3 -> x1, Pallas kernels: 183 us -> 143 us  [on_device(): pl.pallas_call(functools.partial(kernel, n, halves), in_specs=[whole] * 6...]
where the time goes in v2:
time: 184 us
  Pallas kernels  143 us (78%)
  waiting for transfers between devices  22 us (12%)
  starting transfers between devices  8.22 us (4%)
  local copies, waits for them, and re-layouts  5.96 us (3%)
  other arithmetic  3.47 us (2%)
    pallas_call x1, Pallas kernels, on_device(): pl.pallas_call(functools.partial(kernel, n, halves), in_specs=[whole] * 6...  143 us
    ppermute x10, waiting for transfers between devices, scatter_sum(): got = lax.ppermute(give, 'seq', pairs)  22 us
    ppermute x10, starting transfers between devices, scatter_sum(): got = lax.ppermute(give, 'seq', pairs)  8.22 us
  transfers between devices with their start and end apart: 10, of which 7 were waited for; matrix products, arithmetic and copies ran while one was open for 2% of the time, Pallas kernels for 0%

profile of v2, /device:TPU:0, one launch (start us, length us, event | category | flops | bytes accessed | tf_op | source)
XLA Modules:
  0.0 183.9 jit_solution(8983286055269128172)
XLA Ops:
  0.6 143.4 %space_time_backward.1 = (bf16[4,512,384]{2,1,0:T(8,128)(2,1)}, bf16[1152,384]{1,0:T(8,128)(2,1)}, bf16[384,384]{1,0:T(8,128)(2,1)}, bf16[1152,384]{1,0:T(8,128)(2,1)}, bf16[384,384]{1,0:T(8,128)(2,1)}) custom-call(bf16[4,512,384]{2,1,0:T(8,128)(2,1)} %bitcast.80, bf16[4,512,384]{2,1,0:T(8,128)(2,1)} %bitcast.81, bf16[384,1152]{1,0:T(8,128)(2,1)} %wqkv_s_ref.1, ...), custom_call_target="tpu_custom_call" | custom-call | tf_op jit(solution)/shard_map/space_time_backward/pallas_call | solution.py:341
  144.1 0.0 copy-start.3
  144.1 1.3 concatenate.19
  145.4 0.0 copy-done.3
  145.4 0.0 copy-start.1
  145.4 0.1 concatenate.20
  145.5 0.9 fusion.1
  146.4 0.0 copy-start.2
  146.4 0.3 collective-permute-start.5
  146.7 0.0 copy-done.1
  146.7 0.2 concatenate.16
  146.9 0.5 copy-done.2
  147.4 0.1 concatenate.17
  147.5 0.9 fusion.5
  148.4 0.3 collective-permute-start
  148.7 0.0 collective-permute-done.5
  148.7 1.2 convert_add_fusion
  150.0 2.4 %collective-permute-start.6 = (bf16[8,48,384]{2,1,0:T(8,128)(2,1)S(1)}, bf16[8,48,384]{2,1,0:T(8,128)(2,1)S(1)}, u32[]{:S(2)}, u32[]{:S(2)}) collective-permute-start(bf16[8,48,384]{2,1,0:T(8,128)(2,1)S(1)} %fusion.9), channel_id=1, source_target_pairs={{0,2},{1,3},{2,0},{3,1},{4,6},{5,7},{6,4},{7,5},{8,10},{9,11},{10,... | collective-permute-start | bytes 884744 | tf_op jit(solution)/shard_map/ppermute | solution.py:320
  152.5 0.0 collective-permute-done
  152.5 0.2 convert_add_fusion.1
  152.7 0.6 collective-permute-start.1
  153.3 7.0 %collective-permute-done.6 = bf16[8,48,384]{2,1,0:T(8,128)(2,1)S(1)} collective-permute-done((bf16[8,48,384]{2,1,0:T(8,128)(2,1)S(1)}, bf16[8,48,384]{2,1,0:T(8,128)(2,1)S(1)}, u32[]{:S(2)}, u32[]{:S(2)}) %collective-permute-start.6) | collective-permute-done | bytes 294944 | tf_op jit(solution)/shard_map/ppermute | solution.py:320
  160.2 0.1 bitcast_add_fusion
  160.3 2.0 %collective-permute-start.7 = (bf16[4,48,384]{2,1,0:T(8,128)(2,1)S(1)}, bf16[4,48,384]{2,1,0:T(8,128)(2,1)S(1)}, u32[]{:S(2)}, u32[]{:S(2)}) collective-permute-start(bf16[4,48,384]{2,1,0:T(8,128)(2,1)S(1)} %fusion.11), channel_id=1, source_target_pairs={{0,4},{1,5},{2,6},{3,7},{4,0},{5,1},{6,2},{7,3},{8,12},{9,13},{10,... | collective-permute-start | bytes 442376 | tf_op jit(solution)/shard_map/ppermute | solution.py:320
  162.3 4.0 %collective-permute-done.1 = bf16[8,48,384]{2,1,0:T(8,128)(2,1)S(1)} collective-permute-done((bf16[8,48,384]{2,1,0:T(8,128)(2,1)S(1)}, bf16[8,48,384]{2,1,0:T(8,128)(2,1)S(1)}, u32[]{:S(2)}, u32[]{:S(2)}) %collective-permute-start.1) | collective-permute-done | bytes 294944 | tf_op jit(solution)/shard_map/ppermute | solution.py:320
  166.3 0.1 bitcast_add_fusion.1
  166.4 1.5 collective-permute-start.2
  167.9 0.0 collective-permute-done.7
  168.0 0.0 copy-start
  168.0 0.1 collective-permute-start.8
  168.1 4.0 %collective-permute-done.2 = bf16[4,48,384]{2,1,0:T(8,128)(2,1)S(1)} collective-permute-done((bf16[4,48,384]{2,1,0:T(8,128)(2,1)S(1)}, bf16[4,48,384]{2,1,0:T(8,128)(2,1)S(1)}, u32[]{:S(2)}, u32[]{:S(2)}) %collective-permute-start.2) | collective-permute-done | bytes 147488 | tf_op jit(solution)/shard_map/ppermute | solution.py:320
  172.1 0.1 collective-permute-start.3
  172.2 0.2 collective-permute-done.8
  172.4 0.8 collective-permute-start.9
  173.3 3.3 %collective-permute-done.3 = bf16[2,48,384]{2,1,0:T(8,128)(2,1)S(1)} collective-permute-done((bf16[2,48,384]{2,1,0:T(8,128)(2,1)S(1)}, bf16[2,48,384]{2,1,0:T(8,128)(2,1)S(1)}, u32[]{:S(2)}, u32[]{:S(2)}) %collective-permute-start.3) | collective-permute-done | bytes 73760 | tf_op jit(solution)/shard_map/ppermute | solution.py:320
  176.6 0.1 collective-permute-start.4
  176.7 0.7 collective-permute-done.9
  177.4 0.6 slice_bitcast_fusion
  178.0 0.6 slice_bitcast_fusion.2
  178.6 2.9 %collective-permute-done.4 = bf16[1,48,384]{2,1,0:T(8,128)(2,1)S(1)} collective-permute-done((bf16[1,48,384]{2,1,0:T(8,128)(2,1)S(1)}, bf16[1,48,384]{2,1,0:T(8,128)(2,1)S(1)}, u32[]{:S(2)}, u32[]{:S(2)}) %collective-permute-start.4) | collective-permute-done | bytes 36896 | tf_op jit(solution)/shard_map/ppermute | solution.py:320
  181.5 0.6 slice_bitcast_fusion.1
  182.2 0.6 slice_bitcast_fusion.3
  182.8 0.0 copy-done
  182.8 1.1 copy.16
  (14 shorter events, 0.3 us)
Async XLA Ops:
  144.1 1.3 copy-start.3
  145.4 1.4 copy-start.1
  146.4 1.0 copy-start.2
  146.4 2.4 %collective-permute-start.5 = (bf16[16,48,384]{2,1,0:T(8,128)(2,1)}, bf16[16,48,384]{2,1,0:T(8,128)(2,1)}, u32[]{:S(2)}, u32[]{:S(2)}) collective-permute-start(bf16[16,48,384]{2,1,0:T(8,128)(2,1)} %fusion.1), channel_id=1, source_target_pairs={{0,1},{1,0},{2,3},{3,2},{4,5},{5,4},{6,7},{7,6},{8,9},{9,8},{10,11... | collective-permute-start | bytes 1769480 | tf_op jit(solution)/shard_map/ppermute | solution.py:320
  148.4 4.1 %collective-permute-start = (bf16[16,48,384]{2,1,0:T(8,128)(2,1)}, bf16[16,48,384]{2,1,0:T(8,128)(2,1)S(1)}, u32[]{:S(2)}, u32[]{:S(2)}) collective-permute-start(bf16[16,48,384]{2,1,0:T(8,128)(2,1)} %fusion.5), channel_id=1, source_target_pairs={{0,1},{1,0},{2,3},{3,2},{4,5},{5,4},{6,7},{7,6},{8,9},{9,8},{10,11... | collective-permute-start | bytes 1769480 | tf_op jit(solution)/shard_map/ppermute | solution.py:320
  150.0 10.2 %collective-permute-start.6 = (bf16[8,48,384]{2,1,0:T(8,128)(2,1)S(1)}, bf16[8,48,384]{2,1,0:T(8,128)(2,1)S(1)}, u32[]{:S(2)}, u32[]{:S(2)}) collective-permute-start(bf16[8,48,384]{2,1,0:T(8,128)(2,1)S(1)} %fusion.9), channel_id=1, source_target_pairs={{0,2},{1,3},{2,0},{3,1},{4,6},{5,7},{6,4},{7,5},{8,10},{9,11},{10,... | collective-permute-start | bytes 884744 | tf_op jit(solution)/shard_map/ppermute | solution.py:320
  152.7 13.6 %collective-permute-start.1 = (bf16[8,48,384]{2,1,0:T(8,128)(2,1)S(1)}, bf16[8,48,384]{2,1,0:T(8,128)(2,1)S(1)}, u32[]{:S(2)}, u32[]{:S(2)}) collective-permute-start(bf16[8,48,384]{2,1,0:T(8,128)(2,1)S(1)} %fusion.8), channel_id=1, source_target_pairs={{0,2},{1,3},{2,0},{3,1},{4,6},{5,7},{6,4},{7,5},{8,10},{9,11},{10,... | collective-permute-start | bytes 884744 | tf_op jit(solution)/shard_map/ppermute | solution.py:320
  160.3 7.6 %collective-permute-start.7 = (bf16[4,48,384]{2,1,0:T(8,128)(2,1)S(1)}, bf16[4,48,384]{2,1,0:T(8,128)(2,1)S(1)}, u32[]{:S(2)}, u32[]{:S(2)}) collective-permute-start(bf16[4,48,384]{2,1,0:T(8,128)(2,1)S(1)} %fusion.11), channel_id=1, source_target_pairs={{0,4},{1,5},{2,6},{3,7},{4,0},{5,1},{6,2},{7,3},{8,12},{9,13},{10,... | collective-permute-start | bytes 442376 | tf_op jit(solution)/shard_map/ppermute | solution.py:320
  166.4 5.7 %collective-permute-start.2 = (bf16[4,48,384]{2,1,0:T(8,128)(2,1)S(1)}, bf16[4,48,384]{2,1,0:T(8,128)(2,1)S(1)}, u32[]{:S(2)}, u32[]{:S(2)}) collective-permute-start(bf16[4,48,384]{2,1,0:T(8,128)(2,1)S(1)} %fusion.10), channel_id=1, source_target_pairs={{0,4},{1,5},{2,6},{3,7},{4,0},{5,1},{6,2},{7,3},{8,12},{9,13},{10,... | collective-permute-start | bytes 442376 | tf_op jit(solution)/shard_map/ppermute | solution.py:320
  168.0 14.8 %copy-start = (bf16[4,512,384]{2,1,0:T(8,128)(2,1)S(1)}, bf16[4,512,384]{2,1,0:T(8,128)(2,1)}, u32[]{:S(2)}) copy-start(bf16[4,512,384]{2,1,0:T(8,128)(2,1)} %get-tuple-element.10) | copy-start | bytes 4718596
  168.0 4.4 %collective-permute-start.8 = (bf16[2,48,384]{2,1,0:T(8,128)(2,1)S(1)}, bf16[2,48,384]{2,1,0:T(8,128)(2,1)S(1)}, u32[]{:S(2)}, u32[]{:S(2)}) collective-permute-start(bf16[2,48,384]{2,1,0:T(8,128)(2,1)S(1)} %fusion.13), channel_id=1, source_target_pairs={{0,8},{1,9},{2,10},{3,11},{4,12},{5,13},{6,14},{7,15},{8,0},{9,1},... | collective-permute-start | bytes 221192 | tf_op jit(solution)/shard_map/ppermute | solution.py:320
  172.1 4.4 %collective-permute-start.3 = (bf16[2,48,384]{2,1,0:T(8,128)(2,1)S(1)}, bf16[2,48,384]{2,1,0:T(8,128)(2,1)S(1)}, u32[]{:S(2)}, u32[]{:S(2)}) collective-permute-start(bf16[2,48,384]{2,1,0:T(8,128)(2,1)S(1)} %fusion.12), channel_id=1, source_target_pairs={{0,8},{1,9},{2,10},{3,11},{4,12},{5,13},{6,14},{7,15},{8,0},{9,1},... | collective-permute-start | bytes 221192 | tf_op jit(solution)/shard_map/ppermute | solution.py:320
  172.4 4.9 %collective-permute-start.9 = (bf16[1,48,384]{2,1,0:T(8,128)(2,1)S(1)}, bf16[1,48,384]{2,1,0:T(8,128)(2,1)S(1)}, u32[]{:S(2)}, u32[]{:S(2)}) collective-permute-start(bf16[1,48,384]{2,1,0:T(8,128)(2,1)S(1)} %dynamic-slice_convert_fusion.4), channel_id=1, source_target_pairs={{0,16},{1,17},{2,18},{3,19},{4,20},{5,21},{6,22},{7,23},{8,24},{9,... | collective-permute-start | bytes 110600 | tf_op jit(solution)/shard_map/ppermute | solution.py:320
  176.6 4.9 %collective-permute-start.4 = (bf16[1,48,384]{2,1,0:T(8,128)(2,1)S(1)}, bf16[1,48,384]{2,1,0:T(8,128)(2,1)S(1)}, u32[]{:S(2)}, u32[]{:S(2)}) collective-permute-start(bf16[1,48,384]{2,1,0:T(8,128)(2,1)S(1)} %dynamic-slice_convert_fusion.5), channel_id=1, source_target_pairs={{0,16},{1,17},{2,18},{3,19},{4,20},{5,21},{6,22},{7,23},{8,24},{9,... | collective-permute-start | bytes 110600 | tf_op jit(solution)/shard_map/ppermute | solution.py:320
